TPU v7x, 128 devices: a whole 4x4x4 slice. The times are simulated.
128 devices in a mesh: dp: 32 (over z, y, core), tensor: 4 (over x).
Axes of the slice: x: 4, y: 4, z: 4, core: 2. Of those that a mesh axis runs over, the one named last changes fastest.
Arguments:
- tokens: bfloat16 [16384, 768], P('dp'), may hold values from -6 to 6
- cotangent: bfloat16 [16384, 768], P('dp'), may hold values from -6 to 6
- buckets: int32 [256], P('dp'), may hold values from 0 to 1999
- time_table: bfloat16 [2000, 768], replicated, may hold values from -6 to 6
- w_qkv: bfloat16 [2, 768, 3, 768], P(None, None, None, 'tensor'), may hold values from -0.21875 to 0.21875
- w_out: bfloat16 [2, 768, 768], P(None, 'tensor'), may hold values from -1.75 to 1.75
- w_up: bfloat16 [2, 768, 3072], P(None, None, 'tensor'), may hold values from -0.21875 to 0.21875
- w_down: bfloat16 [2, 3072, 768], P(None, 'tensor'), may hold values from -0.15625 to 0.15625
- norm_gain: float32 [2, 2, 768], replicated, may hold values from 0.5 to 1.5
- norm_bias: float32 [2, 2, 768], replicated, may hold values from -3 to 3
Outputs:
- layer_out: bfloat16 [16384, 768], P('dp')
- token_grad: float32 [16384, 768], P('dp')
- table_grad: float32 [2000, 768], P(None, 'tensor')
- qkv_grad: float32 [2, 768, 3, 768], P(None, None, None, 'tensor')
- out_grad: float32 [2, 768, 768], P(None, 'tensor')
- up_grad: float32 [2, 768, 3072], P(None, None, 'tensor')
- down_grad: float32 [2, 3072, 768], P(None, 'tensor')
- gain_grad: float32 [2, 2, 768], replicated
- bias_grad: float32 [2, 2, 768], replicated
All inputs are finite; a program needn't handle non-finite values.
Results may differ from a plain program's by a relative error of at most 0.01.
Values sent between devices are 32-bit elements; how exact they have to be, the bound alone decides.
A program may use at most 128 MiB of HBM per device.

v0:
```python
import jax
import jax.numpy as jnp
from jax import lax
from jax.sharding import PartitionSpec as P

HEAD_DIM = 64
LAYERS = 2
SEQ_LEN = 64


norm_eps = 1e-05


def layer_norm(x, weight_row, shift_row):
    row_mean = jnp.mean(x, axis=-1, keepdims=True)
    centred = x - row_mean
    row_var = jnp.mean(centred * centred, axis=-1, keepdims=True)
    return centred * lax.rsqrt(row_var + norm_eps) * weight_row + shift_row


def attention_local(x, wqkv, wout, gains, shifts):
    row_count = x.shape[0]
    sentence_count = row_count // SEQ_LEN
    local_heads = wqkv.shape[2] // HEAD_DIM
    normed = layer_norm(x, gains[0], shifts[0]).astype(jnp.bfloat16)
    qkv_all = jnp.einsum("rd,dcf->rcf", normed, wqkv, preferred_element_type=jnp.float32).astype(
        jnp.bfloat16
    )
    qkv_heads = qkv_all.reshape(sentence_count, SEQ_LEN, 3, local_heads, HEAD_DIM)
    scores = jnp.einsum(
        "sqhe,skhe->shqk",
        qkv_heads[:, :, 0],
        qkv_heads[:, :, 1],
        preferred_element_type=jnp.float32,
    ) * HEAD_DIM ** (-0.5)
    attn_probs = jax.nn.softmax(scores, axis=-1)
    probs_low = attn_probs.astype(jnp.bfloat16)
    head_mix = jnp.einsum(
        "shqk,skhe->sqhe", probs_low, qkv_heads[:, :, 2], preferred_element_type=jnp.float32
    )
    head_mix = head_mix.reshape(row_count, -1).astype(jnp.bfloat16)
    branch_part = jnp.dot(head_mix, wout, preferred_element_type=jnp.float32)
    return (branch_part, (normed, qkv_heads, attn_probs, probs_low, head_mix))


def mlp_local(hidden, wup, wdown, gains, shifts):
    normed_two = layer_norm(hidden, gains[1], shifts[1]).astype(jnp.bfloat16)
    upward = jnp.dot(normed_two, wup, preferred_element_type=jnp.float32)
    active = jax.nn.gelu(upward).astype(jnp.bfloat16)
    branch_part = jnp.dot(active, wdown, preferred_element_type=jnp.float32)
    return (branch_part, (normed_two, upward, active))


def run_attention(x, wqkv, wout, gains, shifts):
    branch_part, stash_vals = attention_local(x, wqkv, wout, gains, shifts)
    attn_total = lax.psum(branch_part, "tensor")
    return (x + attn_total, attn_total, stash_vals)


def on_device(
    tokens, cotangent, buckets, time_table, w_qkv, w_out, w_up, w_down, norm_gain, norm_bias
):
    row_count = tokens.shape[0]
    sentence_count = row_count // SEQ_LEN
    col_width = w_out.shape[1]
    onehot = (buckets[:, None] == jnp.arange(time_table.shape[0], dtype=jnp.int32)[None, :]).astype(
        jnp.float32
    )
    time_rows = jnp.dot(onehot.astype(jnp.bfloat16), time_table, preferred_element_type=jnp.float32)
    x = tokens.astype(jnp.float32) + jnp.repeat(time_rows, SEQ_LEN, axis=0)
    inputs = []
    kept_sums = []
    for layer_idx in range(LAYERS):
        inputs.append(x)
        hidden, attn_total, unused = run_attention(
            x, w_qkv[layer_idx], w_out[layer_idx], norm_gain[layer_idx], norm_bias[layer_idx]
        )
        kept_sums.append(attn_total)
        mlp_part, unused_two = mlp_local(
            hidden, w_up[layer_idx], w_down[layer_idx], norm_gain[layer_idx], norm_bias[layer_idx]
        )
        x = hidden + lax.psum(mlp_part, "tensor")
    layer_out = x.astype(jnp.bfloat16)
    upstream = cotangent.astype(jnp.float32)
    layer_grads = [None] * LAYERS
    for layer_idx in reversed(range(LAYERS)):
        x = inputs[layer_idx]
        wqkv = w_qkv[layer_idx]
        wout = w_out[layer_idx]
        wup = w_up[layer_idx]
        wdown = w_down[layer_idx]
        gains = norm_gain[layer_idx]
        shifts = norm_bias[layer_idx]
        hidden, unused, stash_vals = run_attention(x, wqkv, wout, gains, shifts)
        unused_part, (normed_two, upward, active) = mlp_local(hidden, wup, wdown, gains, shifts)
        grad_low = upstream.astype(jnp.bfloat16)
        wdown_grad = jnp.einsum("rf,rd->fd", active, grad_low, preferred_element_type=jnp.float32)
        active_grad = jnp.einsum("rd,fd->rf", grad_low, wdown, preferred_element_type=jnp.float32)
        unused_up, gelu_back = jax.vjp(jax.nn.gelu, upward)
        upward_grad = gelu_back(active_grad)[0].astype(jnp.bfloat16)
        wup_grad = jnp.einsum(
            "rd,rf->df", normed_two, upward_grad, preferred_element_type=jnp.float32
        )
        norm_two_part = jnp.einsum(
            "rf,df->rd", upward_grad, wup, preferred_element_type=jnp.float32
        )
        norm_two_grad = lax.psum(norm_two_part, "tensor")
        unused_norm, norm_back_two = jax.vjp(layer_norm, hidden, gains[1], shifts[1])
        hidden_from, gain_two, shift_two = norm_back_two(norm_two_grad)
        hidden_grad = upstream + hidden_from
        normed, qkv_heads, attn_probs, probs_low, head_mix = stash_vals
        local_heads = qkv_heads.shape[3]
        attn_low = hidden_grad.astype(jnp.bfloat16)
        wout_grad = jnp.einsum("rc,rd->cd", head_mix, attn_low, preferred_element_type=jnp.float32)
        mix_grad = jnp.einsum(
            "rd,cd->rc", attn_low, wout, preferred_element_type=jnp.float32
        ).astype(jnp.bfloat16)
        mix_grad = mix_grad.reshape(sentence_count, SEQ_LEN, local_heads, HEAD_DIM)
        value_grad = jnp.einsum(
            "shqk,sqhe->skhe", probs_low, mix_grad, preferred_element_type=jnp.float32
        )
        prob_grad = jnp.einsum(
            "sqhe,skhe->shqk", mix_grad, qkv_heads[:, :, 2], preferred_element_type=jnp.float32
        )
        score_grad = attn_probs * (
            prob_grad - jnp.sum(attn_probs * prob_grad, axis=-1, keepdims=True)
        )
        score_grad = score_grad.astype(jnp.bfloat16)
        query_grad = jnp.einsum(
            "shqk,skhe->sqhe", score_grad, qkv_heads[:, :, 1], preferred_element_type=jnp.float32
        ) * HEAD_DIM ** (-0.5)
        key_grad = jnp.einsum(
            "shqk,sqhe->skhe", score_grad, qkv_heads[:, :, 0], preferred_element_type=jnp.float32
        ) * HEAD_DIM ** (-0.5)
        qkv_grad_rows = jnp.stack([query_grad, key_grad, value_grad], axis=2)
        qkv_grad_rows = qkv_grad_rows.reshape(row_count, 3, -1).astype(jnp.bfloat16)
        wqkv_grad = jnp.einsum(
            "rd,rcf->dcf", normed, qkv_grad_rows, preferred_element_type=jnp.float32
        )
        norm_one_part = jnp.einsum(
            "rcf,dcf->rd", qkv_grad_rows, wqkv, preferred_element_type=jnp.float32
        )
        norm_one_grad = lax.psum(norm_one_part, "tensor")
        unused_norm_one, norm_back_one = jax.vjp(layer_norm, x, gains[0], shifts[0])
        input_from, gain_one, shift_one = norm_back_one(norm_one_grad)
        upstream = hidden_grad + input_from
        grads_here = (
            wqkv_grad,
            wout_grad,
            wup_grad,
            wdown_grad,
            jnp.stack([gain_one, gain_two]),
            jnp.stack([shift_one, shift_two]),
        )
        layer_grads[layer_idx] = grads_here
    col_start = lax.axis_index("tensor") * col_width
    sentence_sums = jnp.sum(upstream.reshape(sentence_count, SEQ_LEN, -1), axis=1)
    sentence_cols = lax.dynamic_slice_in_dim(sentence_sums, col_start, col_width, 1)
    table_local = jnp.einsum("sb,sd->bd", onehot, sentence_cols, precision=lax.Precision.HIGHEST)
    stacked = tuple((jnp.stack([layer_grads[i][j] for i in range(LAYERS)]) for j in range(6)))
    summed = lax.psum(stacked + (table_local,), "dp")
    stacked = summed[:6]
    table_grad = summed[6]
    return (
        layer_out,
        upstream,
        table_grad,
        stacked[0],
        stacked[1],
        stacked[2],
        stacked[3],
        stacked[4],
        stacked[5],
    )


def solution(mesh):
    placed = (
        P("dp", None),
        P("dp", None),
        P("dp"),
        P(),
        P(None, None, None, "tensor"),
        P(None, "tensor", None),
        P(None, None, "tensor"),
        P(None, "tensor", None),
        P(),
        P(),
    )
    return jax.shard_map(
        on_device,
        mesh=mesh,
        in_specs=placed,
        out_specs=(
            P("dp", None),
            P("dp", None),
            P(None, "tensor"),
            P(None, None, None, "tensor"),
            P(None, "tensor", None),
            P(None, None, "tensor"),
            P(None, "tensor", None),
            P(),
            P(),
        ),
        check_vma=False,
    )
```

profile of v0, /device:TPU:1, one launch (start us, length us, event | category | flops | bytes accessed | tf_op | source)
XLA Modules:
  0.0 692.7 jit_solution(14719234729061761301)
XLA Ops:
  7.2 1.8 copy-done
  20.0 53.6 %all-reduce.12.cloned.1.call-done = f32[512,768]{1,0:T(8,128)} async-done(((f32[512,768]{1,0:T(8,128)}), f32[512,768]{1,0:T(8,128)}) %all-reduce.12.cloned.1.call-update) | async-done | bytes 1572880 | tf_op jit(solution)/shard_map/psum | solution.py:56
  73.6 1.8 fusion.172
  77.5 2.2 fusion.48
  79.8 50.6 %all-reduce.14.cloned.1.call-done = f32[512,768]{1,0:T(8,128)} async-done(((f32[512,768]{1,0:T(8,128)}), f32[512,768]{1,0:T(8,128)}) %all-reduce.14.cloned.1.call-update) | async-done | bytes 1572880 | tf_op jit(solution)/shard_map/psum | solution.py:82
  145.9 50.4 %all-reduce.16.cloned.1.call-done = f32[512,768]{1,0:T(8,128)} async-done(((f32[512,768]{1,0:T(8,128)}), f32[512,768]{1,0:T(8,128)}) %all-reduce.16.cloned.1.call-update) | async-done | bytes 1572880 | tf_op jit(solution)/shard_map/psum | solution.py:56
  196.3 2.3 fusion.170
  203.9 2.0 fusion.42
  205.9 50.6 %all-reduce.18.cloned.1.call-done = f32[512,768]{1,0:T(8,128)} async-done(((f32[512,768]{1,0:T(8,128)}), f32[512,768]{1,0:T(8,128)}) %all-reduce.18.cloned.1.call-update) | async-done | bytes 1572880 | tf_op jit(solution)/shard_map/psum | solution.py:107
  256.5 2.7 multiply_reduce_fusion
  264.6 1.9 reshape.228
  266.5 2.6 fusion.30
  269.1 1.8 multiply_reduce_fusion.13
  274.9 1.9 stack.100
  276.8 2.0 copy.62
  278.8 1.9 stack.98
  280.7 2.0 copy.66
  282.7 1.9 stack.99
  288.3 3.1 convolution_bitcast_fusion.5
  291.7 50.4 %all-reduce.20.cloned.1.call-done = f32[512,768]{1,0:T(8,128)} async-done(((f32[512,768]{1,0:T(8,128)}), f32[512,768]{1,0:T(8,128)}) %all-reduce.20.cloned.1.call-update) | async-done | bytes 1572880 | tf_op jit(solution)/shard_map/psum | solution.py:143
  342.1 3.2 multiply_reduce_fusion.1
  352.2 2.0 fusion.52
  354.2 4.0 fusion.38
  358.2 46.6 %all-reduce.22.cloned.1.call-done = f32[512,768]{1,0:T(8,128)} async-done(((f32[512,768]{1,0:T(8,128)}), f32[512,768]{1,0:T(8,128)}) %all-reduce.22.cloned.1.call-update) | async-done | bytes 1572880 | tf_op jit(solution)/shard_map/psum | solution.py:107
  404.8 2.7 multiply_reduce_fusion.2
  411.5 1.9 reshape.229
  413.4 2.5 fusion.31
  416.0 1.8 multiply_reduce_fusion.12
  421.8 1.9 stack.104
  423.8 2.0 copy.75
  425.7 1.9 stack.102
  427.7 2.0 copy.79
  429.6 1.9 stack.103
  435.2 3.2 convolution_bitcast_fusion.4
  438.7 2.3 convolution_bitcast_fusion.2
  445.8 2.7 pad_maximum_fusion
  450.4 2.5 pad_maximum_fusion.1
  455.6 2.1 pad_maximum_fusion.2
  457.7 57.0 %all-reduce.26.cloned.1.call-done = (f32[512,768]{1,0:T(8,128)}, f32[512,768]{1,0:T(8,128)}) async-done(((f32[512,768]{1,0:T(8,128)}, f32[512,768]{1,0:T(8,128)}), (f32[512,768]{1,0:T(8,128)}, f32[512,768]{1,0:T(8,128)})) %all-reduce.26.cloned.1.call-update) | async-done | bytes 3145744 | tf_op jit(solution)/shard_map/psum | solution.py:82
  514.7 2.0 fusion.166
  518.1 1.9 bitcast_reduce_fusion
  520.0 2.1 fusion.99
  523.0 125.3 %all-reduce = (f32[2,2,768]{2,1,0:T(2,128)}, f32[2,2,768]{2,1,0:T(2,128)}) all-reduce(f32[2,2,768]{2,1,0:T(2,128)S(1)} %pad_maximum_fusion.4, f32[2,2,768]{2,1,0:T(2,128)S(1)} %pad_maximum_fusion.5), channel_id=1, replica_groups=mesh['dp'=32,'tensor'=4] {'dp'}, use_global_device_ids=true, to_apply=%region_40.0 | all-reduce | flops 6144 | bytes 49152 | tf_op jit(solution)/shard_map/psum | solution.py:161
  649.3 20.7 %all-reduce.24.cloned.1.call-done = (f32[2000,192]{0,1:T(8,128)}, f32[2,768,3,192]{1,3,2,0:T(8,128)}, f32[2,192,768]{2,1,0:T(8,128)}, f32[2,768,768]{2,1,0:T(8,128)}, f32[2,768,768]{2,1,0:T(8,128)}) async-done(((f32[2000,192]{0,1:T(8,128)}, f32[2,768,3,192]{1,3,2,0:T(8,128)}, f32[2,192,768]{2,1,0:T(8,128)}, f32[2,768,768]{2,1,0:T(8,128)}, f32[2,768,768]{2,1,0:T(8,128)}), (f32[2000,192]{0,1:T(8,128)}, ...) | async-done | bytes 15691792 | tf_op jit(solution)/shard_map/psum | solution.py:161
  670.0 2.9 copy.146
  672.9 4.3 copy.147
  678.3 2.4 copy.149
  681.8 2.4 copy.150
  (348 shorter events, 81.0 us)
Async XLA Ops:
  7.2 66.4 %all-reduce.12.cloned.1.call-start = ((), (), s32[]{:S(2)}) async-start(), calls=%async_computation | async-start | bytes 3145728 | tf_op jit(solution)/shard_map/psum | solution.py:56
  10.4 63.2 %copy-start.29 = (f32[8,768]{1,0:T(8,128)}, f32[8,768]{1,0:T(8,128)S(1)}, u32[]{:S(2)}) copy-start(f32[8,768]{1,0:T(8,128)S(1)} %fusion.100) | copy-start | bytes 73732
  12.8 63.0 %copy-start.92 = (f32[768]{0:T(1024)}, f32[768]{0:T(1024)S(1)}, u32[]{:S(2)}) copy-start(f32[768]{0:T(1024)S(1)} %get-tuple-element.27) | copy-start | bytes 9220
  12.8 119.6 %copy-start.94 = (f32[768]{0:T(1024)}, f32[768]{0:T(1024)S(1)}, u32[]{:S(2)}) copy-start(f32[768]{0:T(1024)S(1)} %get-tuple-element.29) | copy-start | bytes 9220
  15.1 2.2 copy-start.31
  18.4 55.2 %copy-start.6 = (bf16[512,768]{1,0:T(8,128)(2,1)S(1)}, bf16[512,768]{1,0:T(8,128)(2,1)}, u32[]{:S(2)}) copy-start(bf16[512,768]{1,0:T(8,128)(2,1)} %param.10) | copy-start | bytes 2359300
  20.0 110.4 %all-reduce.14.cloned.1.call-start = ((), (), s32[]{:S(2)}) async-start(), calls=%async_computation.1 | async-start | bytes 3145728 | tf_op jit(solution)/shard_map/psum | solution.py:82
  73.6 2.2 copy-start.98
  77.5 2.2 copy-start.104
  79.7 116.6 %all-reduce.16.cloned.1.call-start = ((), (), s32[]{:S(2)}) async-start(), calls=%async_computation.2 | async-start | bytes 3145728 | tf_op jit(solution)/shard_map/psum | solution.py:56
  132.0 2.6 copy-start.2
  132.1 2.6 copy-start.63
  132.4 2.3 copy-start.70
  132.4 2.3 copy-start.75
  138.2 3.0 copy-start.51
  139.9 2.6 copy-start.37
  145.7 110.9 %all-reduce.18.cloned.1.call-start = ((), (), s32[]{:S(2)}) async-start(), calls=%async_computation.3 | async-start | bytes 3145728 | tf_op jit(solution)/shard_map/psum | solution.py:107
  196.3 3.2 copy-start.99
  205.9 136.2 %all-reduce.20.cloned.1.call-start = ((), (), s32[]{:S(2)}) async-start(), calls=%async_computation.4 | async-start | bytes 3145728 | tf_op jit(solution)/shard_map/psum | solution.py:143
  256.5 3.4 copy-start.20
  256.5 3.4 copy-start.57
  291.5 113.4 %all-reduce.22.cloned.1.call-start = ((), (), s32[]{:S(2)}) async-start(), calls=%async_computation.5 | async-start | bytes 3145728 | tf_op jit(solution)/shard_map/psum | solution.py:107
  342.1 3.9 copy-start.3
  342.1 3.9 copy-start.21
  347.7 2.1 copy-start.105
  349.8 2.4 copy-start.100
  354.2 160.5 %all-reduce.26.cloned.1.call-start = ((), (), s32[]{:S(2)}) async-start(), calls=%async_computation.7 | async-start | bytes 6291456 | tf_op jit(solution)/shard_map/psum | solution.py:82
  404.8 2.7 copy-start.69
  404.8 2.8 copy-start.19
  404.8 2.8 copy-start.61
  404.8 2.8 copy-start.73
  438.4 231.7 %all-reduce.24.cloned.1.call-start = ((), (), s32[]{:S(2)}) async-start(), calls=%async_computation.6 | async-start | bytes 31457280 | tf_op jit(solution)/shard_map/psum | solution.py:161
  438.7 2.3 copy-start.25
  438.7 2.3 copy-start.111
  445.8 2.7 copy-start.18
  445.8 3.6 copy-start.106
  450.4 2.5 copy-start.9
  455.6 59.1 %copy-start.7 = (bf16[512,768]{1,0:T(8,128)(2,1)S(1)}, bf16[512,768]{1,0:T(8,128)(2,1)}, u32[]{:S(2)}) copy-start(bf16[512,768]{1,0:T(8,128)(2,1)} %param.10) | copy-start | bytes 2359300
  455.6 59.1 %copy-start.30 = (f32[8,768]{1,0:T(8,128)S(1)}, f32[8,768]{1,0:T(8,128)}, u32[]{:S(2)}) copy-start(f32[8,768]{1,0:T(8,128)} %copy-done.29) | copy-start | bytes 73732
  457.7 59.0 %copy-start.67 = (f32[512]{0:T(512)S(1)}, f32[512]{0:T(512)}, u32[]{:S(2)}) copy-start(f32[512]{0:T(512)} %copy-done.66) | copy-start | bytes 6148
  457.7 59.0 %copy-start.59 = (f32[512]{0:T(512)S(1)}, f32[512]{0:T(512)}, u32[]{:S(2)}) copy-start(f32[512]{0:T(512)} %copy-done.58) | copy-start | bytes 6148
  522.1 126.2 %copy-start.39 = (f32[512,768]{1,0:T(8,128)S(1)}, f32[512,768]{1,0:T(8,128)}, u32[]{:S(2)}) copy-start(f32[512,768]{1,0:T(8,128)} %get-tuple-element.37) | copy-start | bytes 4718596
  670.0 8.2 %slice-start.2 = ((s8[4718592]{0:T(1024)(128)(4,1)}), s8[4194304]{0:T(1024)(128)(4,1)S(1)}, s32[]{:S(2)}) async-start(s8[4718592]{0:T(1024)(128)(4,1)} %bitcast.278), calls=%async_computation.10 | async-start | bytes 8388608
  672.9 4.3 copy-start.44
  672.9 5.3 slice-start.3
  677.2 4.2 slice-start
  678.2 3.5 slice-start.1
  681.8 3.6 copy-start.1
  (76 other events, 100.6 us)
Sparse Core Ops, SparseCore 0:
  20.1 53.4 all-reduce.11
  79.9 50.4 all-reduce.13
  145.8 50.4 all-reduce.15
  206.0 50.4 all-reduce.17
  291.6 50.4 all-reduce.19
  354.3 50.4 all-reduce.21
  438.5 76.1 all-reduce.25
  522.3 147.7 all-reduce.23
where the time goes:
time: 702 us; the launch traced here: 693 us
  waiting for transfers between devices  380 us (54%)
  blocking collectives  125 us (18%)
  local copies, waits for them, and re-layouts  76.8 us (11%)
  matrix products  56 us (8%)
  other arithmetic  37.6 us (5%)
  between operations  15.9 us (2%)
    psum x1, blocking collectives, on_device(): summed = lax.psum(stacked + (table_local,), 'dp')  125 us
    psum x2, waiting for transfers between devices, on_device(): x = hidden + lax.psum(mlp_part, 'tensor')  108 us
    psum x2, waiting for transfers between devices, run_attention(): attn_total = lax.psum(branch_part, 'tensor')  104 us
    psum x2, waiting for transfers between devices, on_device(): norm_two_grad = lax.psum(norm_two_part, 'tensor')  97.2 us
    psum x1, waiting for transfers between devices, on_device(): norm_one_grad = lax.psum(norm_one_part, 'tensor')  50.4 us
    unnamed x245, local copies, waits for them, and re-layouts  42.5 us
    psum x1, waiting for transfers between devices, on_device(): summed = lax.psum(stacked + (table_local,), 'dp')  20.7 us
  transfers between devices with their start and end apart: 8, of which 8 were waited for; matrix products, arithmetic and copies ran while one was open for 3% of the time, Pallas kernels for 0%

commit v1 on v0

v1 whole, which is shorter than its diff:
```python
import functools

import jax
import jax.numpy as jnp
from jax import lax
from jax.experimental import pallas as pl
from jax.experimental.pallas import tpu as pltpu
from jax.sharding import PartitionSpec as P

MESH = pl.DeviceIdType.MESH
F32 = jnp.float32
BF16 = jnp.bfloat16
HEAD_DIM = 64
SEQ_LEN = 64
D = 768
ROWS = 512
BLK = 128
HALF = 64
COLS = 256
EPS = 1e-05
GELU_A = 0.7978845608028654
GELU_B = 0.044715


def nn(a, b):
    return lax.dot_general(a, b, (((1,), (0,)), ((), ())), preferred_element_type=F32)


def nt(a, b):
    return lax.dot_general(a, b, (((1,), (1,)), ((), ())), preferred_element_type=F32)


def tn(a, b):
    return lax.dot_general(a, b, (((0,), (0,)), ((), ())), preferred_element_type=F32)


def norm_parts(x):
    c = x - jnp.mean(x, axis=-1, keepdims=True)
    r = lax.rsqrt(jnp.mean(c * c, axis=-1, keepdims=True) + EPS)
    return c * r, r


def norm(x, g, b):
    return norm_parts(x)[0] * g + b


def norm_back(dn, x, g):
    xh, r = norm_parts(x)
    dx = dn * g
    dx = r * (dx - jnp.mean(dx, axis=-1, keepdims=True) - xh * jnp.mean(dx * xh, axis=-1, keepdims=True))
    return dx, jnp.sum(dn * xh, axis=0, keepdims=True), jnp.sum(dn, axis=0, keepdims=True)


def gelu_cdf(u):
    t = jnp.tanh(GELU_A * (u + GELU_B * (u * u * u)))
    return t, 0.5 + 0.5 * t


def gelu(u):
    return u * gelu_cdf(u)[1]


def gelu_slope(u):
    t, cdf = gelu_cdf(u)
    return cdf + u * (0.5 * (1.0 - t * t)) * (GELU_A * (1.0 + 3.0 * GELU_B * (u * u)))


def body(nz, ny, nx,
         tok_ref, trow_ref, cot_ref, wqkv_ref, wout_ref, wup_ref, wdown_ref, gain_ref, bias_ref,
         lo_ref, tg_ref, gm1_ref, ga1_ref, gm0_ref, ga0_ref, vec_ref,
         ag, sbuf, rh, rf, n1, n2, act, q, k, v, o, u, prob, hs, xs, carry, low, du, dq, dk, dv,
         rs_s, rs_r, ag_s, ag_r):
    dp = lax.axis_index("dp")
    me = lax.axis_index("tensor")
    right = (dp, lax.rem(me + 1, nx))
    left = (dp, lax.rem(me + nx - 1, nx))
    across = (dp, lax.rem(me + 2, nx))

    bar = pltpu.get_barrier_semaphore()
    peers = [right, left]
    for peer in peers:
        pl.semaphore_signal(bar, inc=1, device_id=peer, device_id_type=MESH)
    pl.semaphore_wait(bar, len(peers))

    def rows(b):
        return pl.ds(pl.multiple_of(b * BLK, BLK), BLK)

    def half(b, i):
        return pl.ds(pl.multiple_of(b * BLK + i * HALF, HALF), HALF)

    def turn(rel):
        return lax.rem(me + rel, nx)

    mine = rows(me)

    def rs_copy(i):
        src, dst, to = [
            (sbuf.at[0, 0:HALF], rh.at[0], right),
            (sbuf.at[0, HALF:BLK], rh.at[1], left),
            (sbuf.at[1, HALF:BLK], rf.at[0, HALF:BLK], right),
            (sbuf.at[2, 0:HALF], rf.at[1, 0:HALF], left),
            (sbuf.at[1, 0:HALF], rf.at[0, 0:HALF], right),
            (sbuf.at[2, HALF:BLK], rf.at[1, HALF:BLK], left),
        ][i]
        return pltpu.make_async_remote_copy(
            src_ref=src, dst_ref=dst, send_sem=rs_s.at[i], recv_sem=rs_r.at[i], device_id=to, device_id_type=MESH)

    def rs_send(part):
        def step(j, _):
            blk = turn(jnp.where(j == 0, 2, jnp.where(j == 1, 1, jnp.where(j == 2, 3, 0))))
            for c in range(D // COLS):
                sbuf[j, :, c * COLS:(c + 1) * COLS] = part(rows(blk), c)

            @pl.when(j == 0)
            def _():
                rs_copy(0).start()
                rs_copy(1).start()

            @pl.when(j == 1)
            def _():
                rs_copy(2).start()

            @pl.when(j == 2)
            def _():
                rs_copy(3).start()
                rs_copy(0).wait_recv()
                sbuf[1, 0:HALF] += rh[0]
                rs_copy(4).start()
                rs_copy(1).wait_recv()
                sbuf[2, HALF:BLK] += rh[1]
                rs_copy(5).start()
            return 0
        lax.fori_loop(0, nx, step, 0)

    def rs_done():
        for i in range(2, 6):
            rs_copy(i).wait_recv()
        total = sbuf[3] + rf[0] + rf[1]
        for i in range(6):
            rs_copy(i).wait_send()
        return total

    def ag_copy(i, arriving=False):
        if arriving:
            b, h = [(3, 0), (1, 1), (3, 1), (1, 0), (2, 0), (2, 1)][i]
        else:
            b, h = [(0, 0), (0, 1), (0, 1), (0, 0), (3, 0), (1, 1)][i]
        at = half(turn(b), h)
        return pltpu.make_async_remote_copy(
            src_ref=ag.at[at], dst_ref=ag.at[at], send_sem=ag_s.at[i], recv_sem=ag_r.at[i],
            device_id=[right, left][i % 2], device_id_type=MESH)

    def ag_send(val):
        ag[mine] = val
        for i in range(4):
            ag_copy(i).start()

    def ag_take(fn):
        def step(j, _):
            blk = turn(jnp.where(j == 0, 0, jnp.where(j == 1, 3, jnp.where(j == 2, 1, 2))))

            @pl.when(j == 1)
            def _():
                ag_copy(0, True).wait_recv()
                ag_copy(4).start()
                ag_copy(1, True).wait_recv()
                ag_copy(5).start()
                ag_copy(2, True).wait_recv()

            @pl.when(j == 2)
            def _():
                ag_copy(3, True).wait_recv()

            @pl.when(j == 3)
            def _():
                ag_copy(4, True).wait_recv()
                ag_copy(5, True).wait_recv()
            fn(blk, rows(blk))
            return 0
        lax.fori_loop(0, nx, step, 0)
        for i in range(6):
            ag_copy(i).wait_send()

    def each(fn):
        def step(j, _):
            fn(j, rows(j))
            return 0
        lax.fori_loop(0, nx, step, 0)

    def g_of(l, i):
        return gain_ref[2 * l + i:2 * l + i + 1, :]

    def b_of(l, i):
        return bias_ref[2 * l + i:2 * l + i + 1, :]

    def x0(b, r):
        x = tok_ref[r].astype(F32)
        s = lax.broadcasted_iota(jnp.int32, (BLK, 1), 0) < SEQ_LEN
        return x + jnp.where(s, trow_ref[2 * b], trow_ref[2 * b + 1])

    iq = lax.broadcasted_iota(jnp.int32, (BLK, BLK), 0) // SEQ_LEN
    ik = lax.broadcasted_iota(jnp.int32, (BLK, BLK), 1) // SEQ_LEN
    same = iq == ik
    lane = lax.broadcasted_iota(jnp.int32, (1, BLK), 1) // HEAD_DIM
    heads = [(slice(0, 128), (lane == 0).astype(F32).astype(BF16)), (slice(0, 128), (lane == 1).astype(F32).astype(BF16)),
             (slice(128, 192), None)]

    def only(x, m):
        return x if m is None else x * m

    def attn_out(l, b, r):
        outs = []
        for i, (c, m) in enumerate(heads):
            s = nt(only(q[l, r, c], m), k[l, r, c]) * HEAD_DIM ** -0.5
            s = jnp.where(same, s, -1e30)
            e = jnp.exp(s - jnp.max(s, axis=-1, keepdims=True))
            p = e / jnp.sum(e, axis=-1, keepdims=True)
            prob[l, 3 * b + i] = p
            outs.append(nn(p.astype(BF16), only(v[l, r, c], m)))
        o[l, r, 0:128] = (outs[0] + outs[1]).astype(BF16)
        o[l, r, 128:192] = outs[2].astype(BF16)

    def qkv_attn(l, b, r, n):
        n1[l, r] = n
        for i, t in enumerate((q, k, v)):
            t[l, r, :] = nt(n, wqkv_ref[l, 192 * i:192 * (i + 1), :]).astype(BF16)
        attn_out(l, b, r)

    def attn_back(l, b, r, do):
        got = []
        for i, (c, m) in enumerate(heads):
            p = prob[l, 3 * b + i]
            pb = p.astype(BF16)
            d = only(do[:, c], m)
            dp_ = nt(d, v[l, r, c])
            ds = (p * (dp_ - jnp.sum(p * dp_, axis=-1, keepdims=True))).astype(BF16)
            got.append((nn(ds, only(k[l, r, c], m)), tn(ds, only(q[l, r, c], m)), tn(pb, d)))
        for t, j, s in ((dq, 0, HEAD_DIM ** -0.5), (dk, 1, HEAD_DIM ** -0.5), (dv, 2, 1.0)):
            t[r, 0:128] = ((got[0][j] + got[1][j]) * s).astype(BF16)
            t[r, 128:192] = (got[2][j] * s).astype(BF16)

    def mlp_up(l, r, n):
        n2[l, r] = n
        for c in range(D // COLS):
            cs = slice(c * COLS, (c + 1) * COLS)
            up = nn(n, wup_ref[l, :, cs])
            u[l, r, cs] = up
            act[l, r, cs] = gelu(up).astype(BF16)

    def mlp_back(l, r, gl):
        for c in range(D // COLS):
            cs = slice(c * COLS, (c + 1) * COLS)
            da = nt(gl, wdown_ref[l, cs, :])
            du[r, cs] = (da * gelu_slope(u[l, r, cs])).astype(BF16)

    def weight_grad(a, b, out, wide, at=0):
        for m in range(0, wide, 192):
            for c in range(D // COLS):
                cs = slice(c * COLS, (c + 1) * COLS)
                out[at + m:at + m + 192, cs] = tn(a[:, m:m + 192], b[:, cs])

    def weight_grad_wide(a, b, out):
        def step(i, _):
            at = pl.ds(pl.multiple_of(i * COLS, COLS), COLS)
            for c in range(D // COLS):
                cs = slice(c * COLS, (c + 1) * COLS)
                out[at, cs] = tn(a[:, at], b[:, cs])
            return 0
        lax.fori_loop(0, D // COLS, step, 0)

    def cols(c):
        return slice(c * COLS, (c + 1) * COLS)

    def vec_add(l, i, gg, bg):
        vec_ref[2 * l + i:2 * l + i + 1, :] = gg
        vec_ref[4 + 2 * l + i:5 + 2 * l + i, :] = bg

    def first(b, r):
        qkv_attn(0, b, r, norm(x0(b, r), g_of(0, 0), b_of(0, 0)).astype(BF16))
    each(first)
    x_own = x0(me, mine)
    for l in range(2):
        if l == 1:
            def attn_block(b, r):
                qkv_attn(1, b, r, ag[r].astype(BF16))
            ag_take(attn_block)
        rs_send(lambda r, c, l=l: nn(o[l, r], wout_ref[l, :, cols(c)]))
        h = rs_done() + (x0(me, mine) if l == 0 else xs[...])
        hs[l] = h
        ag_send(norm(h, g_of(l, 1), b_of(l, 1)).astype(BF16).astype(F32))

        def up_block(b, r, l=l):
            mlp_up(l, r, ag[r].astype(BF16))
        ag_take(up_block)
        if l == 0:
            rs_send(lambda r, c: nn(act[0, r], wdown_ref[0, :, cols(c)]))
            x1 = rs_done() + hs[0]
            xs[...] = x1
            ag_send(norm(x1, g_of(1, 0), b_of(1, 0)).astype(BF16).astype(F32))

    carry[...] = cot_ref[mine].astype(F32)
    for l in (1, 0):
        gmat = gm1_ref if l == 1 else gm0_ref
        gatt = ga1_ref if l == 1 else ga0_ref
        if l == 1:
            each(lambda b, r: mlp_back(1, r, cot_ref[r]))
            glow = cot_ref
        else:
            def back_block(b, r):
                gl = ag[r].astype(BF16)
                low[r] = gl
                mlp_back(0, r, gl)
            ag_take(back_block)
            glow = low
        rs_send(lambda r, c, l=l: nt(du[r], wup_ref[l, cols(c), :]))
        weight_grad_wide(act.at[l], glow, gmat.at[1])
        weight_grad_wide(n2.at[l], du, gmat.at[0])
        dx, gg, bg = norm_back(rs_done(), hs[l], g_of(l, 1))
        vec_add(l, 1, gg, bg)
        dh = carry[...] + dx
        carry[...] = dh
        ag_send(dh.astype(BF16).astype(F32))

        def attn_back_block(b, r, l=l):
            dl = ag[r].astype(BF16)
            low[r] = dl
            attn_back(l, b, r, nt(dl, wout_ref[l]).astype(BF16))
        ag_take(attn_back_block)
        rs_send(lambda r, c, l=l: nn(dq[r], wqkv_ref[l, 0:192, cols(c)]) + nn(dk[r], wqkv_ref[l, 192:384, cols(c)])
                + nn(dv[r], wqkv_ref[l, 384:576, cols(c)]))
        for i, t in enumerate((dq, dk, dv)):
            weight_grad(t, n1.at[l], gatt.at[0], 192, 192 * i)
        weight_grad(o.at[l], low, gatt.at[0], 192, 576)
        dx, gg, bg = norm_back(rs_done(), xs[...] if l == 1 else x0(me, mine), g_of(l, 0))
        vec_add(l, 0, gg, bg)
        g = carry[...] + dx
        carry[...] = g
        if l == 1:
            ag_send(g.astype(BF16).astype(F32))
    ag_send(carry[...])

    def grad_block(b, r):
        tg_ref[r] = ag[r]
    ag_take(grad_block)

    rs_send(lambda r, c: nn(act[1, r], wdown_ref[1, :, cols(c)]))
    ag_send((rs_done() + hs[1]).astype(BF16).astype(F32))

    def out_block(b, r):
        lo_ref[r] = ag[r].astype(BF16)
    ag_take(out_block)


def on_device(nz, ny, nx, tokens, cotangent, buckets, time_table, w_qkv, w_out, w_up, w_down, norm_gain, norm_bias):
    trow = jnp.take(time_table, buckets, axis=0).astype(F32).reshape(-1, 1, D)
    wqkv = w_qkv.transpose(0, 2, 3, 1).reshape(2, -1, D)
    vm = pl.BlockSpec(memory_space=pltpu.VMEM)
    sd = jax.ShapeDtypeStruct
    sem = pltpu.SemaphoreType.DMA
    out = pl.pallas_call(
        functools.partial(body, nz, ny, nx),
        out_shape=(sd((ROWS, D), BF16), sd((ROWS, D), F32), sd((2, D, D), F32), sd((1, D, D), F32),
                   sd((2, D, D), F32), sd((1, D, D), F32), sd((8, D), F32)),
        in_specs=[vm] * 9,
        out_specs=(vm,) * 7,
        scratch_shapes=[
            pltpu.VMEM((ROWS, D), F32),
            pltpu.VMEM((4, BLK, D), F32),
            pltpu.VMEM((2, HALF, D), F32),
            pltpu.VMEM((2, BLK, D), F32),
            pltpu.VMEM((2, ROWS, D), BF16),
            pltpu.VMEM((2, ROWS, D), BF16),
            pltpu.VMEM((2, ROWS, D), BF16),
            pltpu.VMEM((2, ROWS, 192), BF16),
            pltpu.VMEM((2, ROWS, 192), BF16),
            pltpu.VMEM((2, ROWS, 192), BF16),
            pltpu.VMEM((2, ROWS, 192), BF16),
            pltpu.VMEM((2, ROWS, D), F32),
            pltpu.VMEM((2, 12, BLK, BLK), F32),
            pltpu.VMEM((2, BLK, D), F32),
            pltpu.VMEM((BLK, D), F32),
            pltpu.VMEM((BLK, D), F32),
            pltpu.VMEM((ROWS, D), BF16),
            pltpu.VMEM((ROWS, D), BF16),
            pltpu.VMEM((ROWS, 192), BF16),
            pltpu.VMEM((ROWS, 192), BF16),
            pltpu.VMEM((ROWS, 192), BF16),
            sem((6,)), sem((6,)), sem((6,)), sem((6,)),
        ],
        compiler_params=pltpu.CompilerParams(collective_id=0, has_side_effects=True, vmem_limit_bytes=60 * 2 ** 20),
        name="layers",
    )(tokens, trow, cotangent, wqkv, w_out, w_up, w_down, norm_gain.reshape(4, D), norm_bias.reshape(4, D))
    lo, tg, gm1, ga1, gm0, ga0, vec = out
    mats = jnp.concatenate([ga0, gm0, ga1, gm1])
    mats = lax.psum(mats, "dp")
    vec = lax.psum(vec, ("dp", "tensor"))
    col = lax.axis_index("tensor") * 192
    sums = jnp.sum(tg.reshape(-1, SEQ_LEN, D), axis=1)
    sums = lax.dynamic_slice_in_dim(sums, col, 192, 1)
    sums = lax.all_gather(sums, "dp", axis=0, tiled=True)
    ids = lax.all_gather(buckets, "dp", axis=0, tiled=True)
    onehot = (ids[:, None] == jnp.arange(time_table.shape[0], dtype=jnp.int32)[None, :]).astype(F32)
    table = jnp.einsum("sb,sd->bd", onehot, sums, precision=lax.Precision.HIGHEST)
    att = jnp.stack([mats[0], mats[3]])
    up = jnp.stack([mats[1], mats[4]])
    down = jnp.stack([mats[2], mats[5]])
    qkv = att[:, 0:576].reshape(2, 3, 192, D).transpose(0, 3, 1, 2)
    return (lo, tg, table, qkv, att[:, 576:768], up, down, vec[0:4].reshape(2, 2, D), vec[4:8].reshape(2, 2, D))


def solution(mesh):
    placed = (
        P("dp", None), P("dp", None), P("dp"), P(), P(None, None, None, "tensor"), P(None, "tensor", None),
        P(None, None, "tensor"), P(None, "tensor", None), P(), P(),
    )
    return jax.shard_map(
        functools.partial(on_device, 4, 4, 4),
        mesh=mesh,
        in_specs=placed,
        out_specs=(
            P("dp", None), P("dp", None), P(None, "tensor"), P(None, None, None, "tensor"), P(None, "tensor", None),
            P(None, None, "tensor"), P(None, "tensor", None), P(), P(),
        ),
        check_vma=False,
    )
```

time: 702 us -> 443 us (0.63); the launches traced: 693 us -> 443 us
  waiting for transfers between devices: 380 us -> 30.1 us
  Pallas kernels: 0 us -> 235 us
  local copies, waits for them, and re-layouts: 76.8 us -> 21 us
  matrix products: 56 us -> 2.25 us
  other arithmetic: 37.6 us -> 21.6 us
    psum x8 -> x1, waiting for transfers between devices: 380 us -> 30.1 us  [on_device(): mats = lax.psum(mats, 'dp')]
    pallas_call x0 -> x1, Pallas kernels: none -> 235 us  [on_device(): pl.pallas_call(functools.partial(body, nz, ny, nx), out_shape=(sd((ROWS,...]
    dot_general x32 -> x1, matrix products: 50.5 us -> 2.25 us  [on_device(): jnp.einsum('sb,sd->bd', onehot, sums, precision=lax.Precision.HIGHEST)]
    psum x1, blocking collectives: 125 us -> 79.3 us  [on_device(): vec = lax.psum(vec, ('dp', 'tensor'))]
    unnamed x245 -> x31, local copies, waits for them, and re-layouts: 42.5 us -> 6.83 us
    all_gather x0 -> x1, blocking collectives: none -> 27.7 us  [on_device(): sums = lax.all_gather(sums, 'dp', axis=0, tiled=True)]
    reduce_sum x17 -> x1, other arithmetic: 24.2 us -> 0.12 us  [on_device(): sums = jnp.sum(tg.reshape(-1, SEQ_LEN, D), axis=1)]
    another operation x8 -> x0, local copies, waits for them, and re-layouts: 13.5 us -> none  [on_device(): qkv_grad_rows = jnp.stack([query_grad, key_grad, value_grad], axis=2)]
  transfers between devices with their start and end apart: 8 -> 1, of which waited for: 8 -> 1; matrix products, arithmetic and copies ran while one was open for 3% -> 1% of each run, Pallas kernels for 0% -> 0%
where the time goes in v1:
time: 443 us
  Pallas kernels  235 us (53%)
  blocking collectives  118 us (27%)
  waiting for transfers between devices  30.1 us (7%)
  other arithmetic  21.6 us (5%)
  local copies, waits for them, and re-layouts  21 us (5%)
  between operations  14.8 us (3%)
    pallas_call x1, Pallas kernels, on_device(): pl.pallas_call(functools.partial(body, nz, ny, nx), out_shape=(sd((ROWS,...  235 us
    psum x1, blocking collectives, on_device(): vec = lax.psum(vec, ('dp', 'tensor'))  79.3 us
    psum x1, waiting for transfers between devices, on_device(): mats = lax.psum(mats, 'dp')  30.1 us
    all_gather x1, blocking collectives, on_device(): sums = lax.all_gather(sums, 'dp', axis=0, tiled=True)  27.7 us
    unnamed x1, blocking collectives  11.1 us
    concatenate x1, other arithmetic, on_device(): mats = jnp.concatenate([ga0, gm0, ga1, gm1])  10.5 us
    slice x1, local copies, waits for them, and re-layouts, on_device(): down = jnp.stack([mats[2], mats[5]])  9.64 us
  transfers between devices with their start and end apart: 1, of which 1 were waited for; matrix products, arithmetic and copies ran while one was open for 1% of the time, Pallas kernels for 0%

profile of v1, /device:TPU:1, one launch (start us, length us, event | category | flops | bytes accessed | tf_op | source)
XLA Modules:
  0.0 442.9 jit_solution(8673172048716298187)
XLA Ops:
  7.2 0.0 copy-start
  7.2 0.0 all-reduce.3.cloned.1.call-start
  7.2 0.8 compare_select_fusion
  8.0 0.7 compare_and_fusion
  8.8 1.3 reshape.74.gain_ref
  10.1 1.3 reshape.75.bias_ref
  11.4 0.0 copy-done
  11.4 0.6 gather_fusion
  12.0 0.7 fusion.3.trow_ref
  12.7 235.0 %layers.1 = (bf16[512,768]{1,0:T(8,128)(2,1)}, f32[512,768]{1,0:T(8,128)}, f32[2,768,768]{2,1,0:T(8,128)}, f32[1,768,768]{2,1,0:T(8,128)}, f32[2,768,768]{2,1,0:...) custom-call(bf16[512,768]{1,0:T(8,128)(2,1)} %tok_ref.1, f32[8,1,768]{2,1,0:T(1,128)} %fusion.3.trow_ref, ...), custom_call_target="tpu_custom_call" | custom-call | tf_op jit(solution)/shard_map/layers/pallas_call | solution.py:360
  247.8 10.5 %pad_maximum_fusion = f32[6,768,768]{2,1,0:T(8,128)} fusion(f32[2,768,768]{2,1,0:T(8,128)} %get-tuple-element.21, f32[1,768,768]{2,1,0:T(8,128)} %get-tuple-element.20, f32[2,768,768]{2,1,0:T(8,128)} %get-tuple-element.19, f32[1,768,768]{2,1,0:T(8,128)} %get-tuple-element.18), kind=kLoop, calls=%fused_computation.1 | loop fusion | flops 10616832 | bytes 28311552 | tf_op jit(solution)/shard_map/concatenate | solution.py:394
  258.3 0.0 copy-start.10
  258.3 0.0 copy-start.12
  258.3 0.0 copy-start.11
  258.3 0.0 copy-start.7
  258.3 0.0 all-reduce.3.cloned.1.call-update
  258.3 0.7 copy-done.10
  259.0 79.3 %psum.15 = f32[8,768]{1,0:T(8,128)S(1)} all-reduce(f32[8,768]{1,0:T(8,128)S(1)} %copy-done.10), channel_id=1, replica_groups=mesh['dp'=32,'tensor'=4] {'dp','tensor'}, use_global_device_ids=true, to_apply=%region_2.3 | all-reduce | flops 6144 | bytes 49152 | tf_op jit(solution)/shard_map/psum | solution.py:396
  338.4 0.6 reshape.78
  339.0 0.6 reshape.79
  339.6 0.0 copy-done.12
  339.6 0.6 dynamic-slice
  340.8 0.0 copy-done.11
  340.8 0.2 dynamic-update-slice
  341.1 11.1 %all-reduce = s32[256]{0:T(256)S(1)} all-reduce(s32[256]{0:T(256)S(1)} %dynamic-update-slice), channel_id=1, replica_groups=mesh['dp'=32,'tensor'=4] {'dp'}, use_global_device_ids=true, to_apply=%add | all-reduce | flops 256 | bytes 2048
  352.2 0.0 copy-done.7
  352.2 0.1 bitcast_reduce_fusion
  352.3 0.1 constant_dynamic-slice_fusion
  352.4 27.7 %all_gather.7 = f32[256,192]{1,0:T(8,128)S(1)} all-gather(f32[8,192]{1,0:T(8,128)S(1)} %constant_dynamic-slice_fusion), channel_id=1, replica_groups=mesh['dp'=32,'tensor'=4] {'dp'}, dimensions={0}, use_global_device_ids=true | all-gather | bytes 202752 | tf_op jit(solution)/shard_map/all_gather | solution.py:400
  380.1 2.3 fusion.1
  382.3 30.1 %all-reduce.3.cloned.1.call-done = f32[6,768,768]{2,1,0:T(8,128)} async-done(((f32[6,768,768]{2,1,0:T(8,128)}), f32[6,768,768]{2,1,0:T(8,128)}) %all-reduce.3.cloned.1.call-update) | async-done | bytes 14155792 | tf_op jit(solution)/shard_map/psum | solution.py:395
  412.4 9.6 %fusion.4 = (f32[1,768,768]{2,1,0:T(8,128)}, f32[1,768,768]{2,1,0:T(8,128)}, f32[1,768,768]{2,1,0:T(8,128)}, f32[1,768,768]{2,1,0:T(8,128)}, f32[1,768,768]{2,1,0:T(8,128)S(1)}, /*index=5*/f32[1,768,768]{2,1,0:T(8,128)}) fusion(f32[6,768,768]{2,1,0:T(8,128)} %all-reduce.3.cloned.1.call-done), kind=kLoop, calls=%fused_computation.18 | loop fusion | bytes 28311552 | tf_op jit(solution)/shard_map/slice | solution.py:406
  422.1 0.0 copy-start.2
  422.1 0.0 copy-start.6
  422.1 2.3 pad_maximum_fusion.3
  424.4 0.0 copy-done.2
  424.4 0.0 copy-start.3
  424.4 2.0 fusion
  426.4 0.0 copy-done.6
  426.4 0.9 copy-done.3
  427.3 0.8 copy-done.4
  428.2 0.7 copy-done.5
  428.9 4.3 pad_maximum_fusion.1
  433.2 0.0 copy-done.9
  433.2 0.9 copy.27
  434.1 0.8 copy-done.8
  434.9 1.1 copy.28
  436.0 0.0 copy-done.1
  (8 shorter events, 0.0 us)
Async XLA Ops:
  7.2 4.3 copy-start
  7.2 405.2 %all-reduce.3.cloned.1.call-start = ((), (), s32[]{:S(2)}) async-start(), calls=%async_computation | async-start | bytes 28311552 | tf_op jit(solution)/shard_map/psum | solution.py:395
  258.3 0.7 copy-start.10
  258.3 81.3 %copy-start.12 = (u32[128]{0:T(128)S(1)}, u32[128]{0:T(128)}, u32[]{:S(2)}) copy-start(u32[128]{0:T(128)} %constant.30) | copy-start | bytes 1540
  258.3 82.5 %copy-start.11 = (s32[8]{0:T(128)S(1)}, s32[8]{0:T(128)}, u32[]{:S(2)}) copy-start(s32[8]{0:T(128)} %param.12) | copy-start | bytes 100
  258.3 93.9 %copy-start.7 = (f32[512,768]{1,0:T(8,128)S(1)}, f32[512,768]{1,0:T(8,128)}, u32[]{:S(2)}) copy-start(f32[512,768]{1,0:T(8,128)} %get-tuple-element.43) | copy-start | bytes 4718596
  422.1 2.3 copy-start.2
  422.1 4.4 copy-start.6
  424.4 3.0 copy-start.3
  424.4 3.8 copy-start.4
  424.4 4.5 %copy-start.5 = (f32[1,768,768]{2,1,0:T(8,128)S(1)}, f32[1,768,768]{2,1,0:T(8,128)}, u32[]{:S(2)}) copy-start(f32[1,768,768]{2,1,0:T(8,128)} %get-tuple-element.25) | copy-start | bytes 7077892
  428.9 4.4 copy-start.9
  433.2 1.7 copy-start.8
  433.2 2.8 copy-start.1
Sparse Core Ops, SparseCore 0:
  258.5 153.9 all-reduce.2

commit v2 on v1

--- a/solution.py
+++ b/solution.py
@@ -66,18 +66,29 @@
 
 
 def body(nz, ny, nx,
-         tok_ref, trow_ref, cot_ref, wqkv_ref, wout_ref, wup_ref, wdown_ref, gain_ref, bias_ref,
-         lo_ref, tg_ref, gm1_ref, ga1_ref, gm0_ref, ga0_ref, vec_ref,
-         ag, sbuf, rh, rf, n1, n2, act, q, k, v, o, u, prob, hs, xs, carry, low, du, dq, dk, dv,
-         rs_s, rs_r, ag_s, ag_r):
+         tok_ref, trow_ref, cot_ref, ids_ref, wqkv_ref, wout_ref, wup_ref, wdown_ref, gain_ref, bias_ref,
+         lo_ref, tg_ref, table_ref, gain_out, bias_out, att_out, mlp_out,
+         gm1_ref, ga1_ref, gm0_ref, ga0_ref, vec_ref, ag, sbuf, rh, rf, n1, n2, act, q, k, v, o, u, prob, hs, xs, carry, low, du, dq, dk, dv,
+         core_m, half_m, full_m, sub_m, core_a, half_a, full_a, sub_a, vecs, ids_all, sums_all,
+         rs_s, rs_r, ag_s, ag_r, sm_s, sm_r, sa_s, sa_r, sv_s, sv_r, si_s, si_r, st_s, st_r, km_s, ka_s):
     dp = lax.axis_index("dp")
     me = lax.axis_index("tensor")
+    core = lax.rem(dp, 2)
+    y = lax.rem(dp // 2, ny)
+    z = dp // (2 * ny)
     right = (dp, lax.rem(me + 1, nx))
     left = (dp, lax.rem(me + nx - 1, nx))
-    across = (dp, lax.rem(me + 2, nx))
+
+    def at(zz, yy, cc):
+        return ((lax.rem(zz, nz) * ny + lax.rem(yy, ny)) * 2 + lax.rem(cc, 2), me)
+
+    def along(axis, o):
+        return at(z, y + o, core) if axis == 0 else at(z + o, y, core)
+
+    twin = at(z, y, core + 1)
 
     bar = pltpu.get_barrier_semaphore()
-    peers = [right, left]
+    peers = [(dp, lax.rem(me + i, nx)) for i in (1, 2, 3)] + [along(a, i) for a in (0, 1) for i in (1, 2, 3)] + [twin]
     for peer in peers:
         pl.semaphore_signal(bar, inc=1, device_id=peer, device_id_type=MESH)
     pl.semaphore_wait(bar, len(peers))
@@ -188,10 +199,10 @@
         lax.fori_loop(0, nx, step, 0)
 
     def g_of(l, i):
-        return gain_ref[2 * l + i:2 * l + i + 1, :]
+        return gain_ref[l, i:i + 1, :]
 
     def b_of(l, i):
-        return bias_ref[2 * l + i:2 * l + i + 1, :]
+        return bias_ref[l, i:i + 1, :]
 
     def x0(b, r):
         x = tok_ref[r].astype(F32)
@@ -275,6 +286,225 @@
         vec_ref[2 * l + i:2 * l + i + 1, :] = gg
         vec_ref[4 + 2 * l + i:5 + 2 * l + i, :] = bg
 
+    def remote(src, dst, sems, i, to):
+        return pltpu.make_async_remote_copy(
+            src_ref=src, dst_ref=dst, send_sem=sems[0].at[i], recv_sem=sems[1].at[i], device_id=to, device_id_type=MESH)
+
+    def add_into(mat, n, row, count, cs, srcs, unit=48):
+        unit = min(unit, count)
+
+        def step(i, _):
+            for kk in range(n):
+                to = pl.ds(pl.multiple_of(row + i * unit, 8), unit)
+                fr = pl.ds(pl.multiple_of(i * unit, 8), unit)
+                acc = mat[kk, to, cs]
+                for src in srcs:
+                    acc = acc + src[kk, fr, :]
+                mat[kk, to, cs] = acc
+            return 0
+        if count == unit:
+            step(0, 0)
+        else:
+            lax.fori_loop(0, count // unit, step, 0)
+
+    def all_sum(mat, res, n, core_b, half_b, full_b, sub_b, sems):
+        mine_at = core * 384
+        first = (y, z)
+        second = (z, y)
+        cs = (slice(0, 384), slice(384, 768))
+
+        def blk(p, o, h=0):
+            return mine_at + lax.rem(first[p] + o, 4) * 96 + h * 48
+
+        def sub(p, o):
+            return blk(p, 0) + lax.rem(second[p] + o, 4) * 24
+
+        def part(p, row, count, of=mat):
+            return of.at[:, pl.ds(pl.multiple_of(row, 8), count), cs[p]]
+
+        def copy(p, i):
+            s_ = 2 + 18 * p + i
+            r_, l_ = along(p, 1), along(p, 3)
+            if i < 6:
+                src, dst, to = [
+                    (part(p, blk(p, 2, 0), 48), half_b.at[p, 0], r_),
+                    (part(p, blk(p, 2, 1), 48), half_b.at[p, 1], l_),
+                    (part(p, blk(p, 1, 1), 48), full_b.at[p, 0, :, 48:96], r_),
+                    (part(p, blk(p, 3, 0), 48), full_b.at[p, 1, :, 0:48], l_),
+                    (part(p, blk(p, 1, 0), 48), full_b.at[p, 0, :, 0:48], r_),
+                    (part(p, blk(p, 3, 1), 48), full_b.at[p, 1, :, 48:96], l_),
+                ][i]
+            elif i < 9:
+                o_ = i - 5
+                src, dst, to = part(p, sub(p, o_), 24), sub_b.at[p, o_ - 1], along(1 - p, o_)
+            elif i < 12:
+                src, dst = part(p, sub(p, 0), 24), part(p, sub(p, 0), 24, res)
+                to = along(1 - p, i - 8)
+            else:
+                b, h, to = [(0, 0, r_), (0, 1, l_), (0, 1, r_), (0, 0, l_), (3, 0, r_), (1, 1, l_)][i - 12]
+                src = dst = part(p, blk(p, b, h), 48, res)
+            return remote(src, dst, sems, s_, to)
+
+        def landing(p, i):
+            if i < 9:
+                return copy(p, i)
+            if i < 12:
+                ref = part(p, sub(p, 12 - i), 24, res)
+            else:
+                b, h = [(3, 0), (1, 1), (3, 1), (1, 0), (2, 0), (2, 1)][i - 12]
+                ref = part(p, blk(p, b, h), 48, res)
+            return remote(ref, ref, sems, 2 + 18 * p + i, along(p, 1))
+
+        def own(o, of=mat):
+            return of.at[:, pl.ds(pl.multiple_of(lax.rem(core + o, 2) * 384, 8), 384), :]
+
+        def keep(p):
+            return pltpu.make_async_copy(part(p, sub(p, 0), 24), part(p, sub(p, 0), 24, res), sems[2].at[p])
+
+        c0 = remote(own(1), core_b, sems, 0, twin)
+        c0.start()
+        yield
+        c0.wait_recv()
+        add_into(mat, n, mine_at, 384, slice(0, 768), [core_b])
+        for i in range(4):
+            for p in (0, 1):
+                copy(p, i).start()
+        yield
+        for p in (0, 1):
+            landing(p, 0).wait_recv()
+            add_into(mat, n, blk(p, 1, 0), 48, cs[p], [half_b.at[p, 0]])
+            copy(p, 4).start()
+            landing(p, 1).wait_recv()
+            add_into(mat, n, blk(p, 3, 1), 48, cs[p], [half_b.at[p, 1]])
+            copy(p, 5).start()
+        yield
+        for p in (0, 1):
+            for i in (2, 3, 4, 5):
+                landing(p, i).wait_recv()
+            add_into(mat, n, blk(p, 0), 96, cs[p], [full_b.at[p, 0], full_b.at[p, 1]])
+            for i in (6, 7, 8):
+                copy(p, i).start()
+        c0.wait_send()
+        yield
+        for p in (0, 1):
+            for i in (6, 7, 8):
+                landing(p, i).wait_recv()
+            add_into(mat, n, sub(p, 0), 24, cs[p], [sub_b.at[p, 0], sub_b.at[p, 1], sub_b.at[p, 2]])
+            for i in (9, 10, 11):
+                copy(p, i).start()
+            keep(p).start()
+            for i in range(9):
+                copy(p, i).wait_send()
+        yield
+        for p in (0, 1):
+            keep(p).wait()
+            for i in (9, 10, 11):
+                landing(p, i).wait_recv()
+            for i in (12, 13, 14, 15):
+                copy(p, i).start()
+        yield
+        for p in (0, 1):
+            landing(p, 12).wait_recv()
+            copy(p, 16).start()
+            landing(p, 13).wait_recv()
+            copy(p, 17).start()
+        yield
+        for p in (0, 1):
+            for i in (14, 15, 16, 17):
+                landing(p, i).wait_recv()
+        c1 = remote(own(0, res), own(0, res), sems, 1, twin)
+        c1.start()
+        for p in (0, 1):
+            for i in range(9, 18):
+                copy(p, i).wait_send()
+        yield
+        remote(own(1, res), own(1, res), sems, 1, twin).wait_recv()
+        c1.wait_send()
+
+    running = []
+
+    def tick():
+        for t in list(running):
+            if next(t, True):
+                running.remove(t)
+
+    def finish(t):
+        while t in running:
+            if next(t, True):
+                running.remove(t)
+
+    def spread(buf, sems):
+        def group(i):
+            if i < 3:
+                return buf.at[z, y, core], along(1, i + 1), lambda: buf.at[lax.rem(z + 3 - i, 4), y, core]
+            if i < 6:
+                return buf.at[:, y, core], along(0, i - 2), lambda: buf.at[:, lax.rem(y + 6 - i, 4), core]
+            return buf.at[:, :, core], twin, lambda: buf.at[:, :, lax.rem(core + 1, 2)]
+
+        for some in ((0, 1, 2), (3, 4, 5), (6,)):
+            for i in some:
+                src, to, _ = group(i)
+                remote(src, src, sems, i, to).start()
+            yield
+            for i in some:
+                src, to, where = group(i)
+                remote(where(), where(), sems, i, to).wait_recv()
+            for i in some:
+                src, to, _ = group(i)
+                remote(src, src, sems, i, to).wait_send()
+
+    def sum_vecs():
+        val = vec_ref[...]
+        i = 0
+        for stage, (pos, peers_) in enumerate((
+                (me, [(dp, lax.rem(me + i_, nx)) for i_ in (1, 2, 3)]),
+                (z, [along(1, i_) for i_ in (1, 2, 3)]),
+                (y, [along(0, i_) for i_ in (1, 2, 3)]),
+                (core, [twin]))):
+            count = len(peers_) + 1
+            buf = vecs.at[stage]
+            buf[pos] = val
+            sent = []
+            for j, to in enumerate(peers_):
+                cp = remote(buf.at[pos], buf.at[pos], (sv_s, sv_r), i + j, to)
+                cp.start()
+                sent.append(cp)
+            yield
+            for j in range(len(peers_)):
+                ref = buf.at[lax.rem(pos + count - 1 - j, count)]
+                remote(ref, ref, (sv_s, sv_r), i + j, twin).wait_recv()
+            for cp in sent:
+                cp.wait_send()
+            i += len(peers_)
+            val = buf[0]
+            for j in range(1, count):
+                val = val + buf[j]
+        for l in range(2):
+            for w in range(2):
+                gain_out[l, w:w + 1, :] = val[2 * l + w:2 * l + w + 1, :]
+                bias_out[l, w:w + 1, :] = val[4 + 2 * l + w:5 + 2 * l + w, :]
+
+    def table_sums():
+        bound = table_ref.shape[1]
+        ids = ids_all[...].reshape(256, BLK)[:, 0:1]
+        rest = jnp.zeros((256, 192), F32)
+        flat = sums_all[...].reshape(256, D)
+        for t in range(4):
+            rest = jnp.where(me == t, flat[:, 192 * t:192 * (t + 1)], rest)
+        parts = []
+        for _ in range(3):
+            top = rest.astype(BF16)
+            parts.append(top)
+            rest = rest - top.astype(F32)
+        for c in range(0, bound, 512):
+            w = min(512, bound - c)
+            hot = lax.broadcasted_iota(jnp.int32, (256, w), 1).astype(F32) + float(c) == ids
+            hot = hot.astype(F32).astype(BF16)
+            table_ref[:, c:c + w] = tn(parts[0], hot) + (tn(parts[1], hot) + tn(parts[2], hot))
+
+    ids_all[z, y, core] = ids_ref[...].astype(F32)
+    running.append(spread(ids_all, (si_s, si_r)))
+    tick()
     def first(b, r):
         qkv_attn(0, b, r, norm(x0(b, r), g_of(0, 0), b_of(0, 0)).astype(BF16))
     each(first)
@@ -299,6 +529,7 @@
             ag_send(norm(x1, g_of(1, 0), b_of(1, 0)).astype(BF16).astype(F32))
 
     carry[...] = cot_ref[mine].astype(F32)
+    mlp_sum = att_sum = None
     for l in (1, 0):
         gmat = gm1_ref if l == 1 else gm0_ref
         gatt = ga1_ref if l == 1 else ga0_ref
@@ -312,58 +543,102 @@
                 mlp_back(0, r, gl)
             ag_take(back_block)
             glow = low
+        tick()
         rs_send(lambda r, c, l=l: nt(du[r], wup_ref[l, cols(c), :]))
+        tick()
         weight_grad_wide(act.at[l], glow, gmat.at[1])
         weight_grad_wide(n2.at[l], du, gmat.at[0])
+        finish(mlp_sum)
+        mlp_sum = all_sum(gmat, mlp_out.at[l], 2, core_m, half_m, full_m, sub_m, (sm_s, sm_r, km_s))
+        running.append(mlp_sum)
+        tick()
         dx, gg, bg = norm_back(rs_done(), hs[l], g_of(l, 1))
         vec_add(l, 1, gg, bg)
         dh = carry[...] + dx
         carry[...] = dh
         ag_send(dh.astype(BF16).astype(F32))
+        tick()
 
         def attn_back_block(b, r, l=l):
             dl = ag[r].astype(BF16)
             low[r] = dl
             attn_back(l, b, r, nt(dl, wout_ref[l]).astype(BF16))
         ag_take(attn_back_block)
+        tick()
         rs_send(lambda r, c, l=l: nn(dq[r], wqkv_ref[l, 0:192, cols(c)]) + nn(dk[r], wqkv_ref[l, 192:384, cols(c)])
                 + nn(dv[r], wqkv_ref[l, 384:576, cols(c)]))
+        tick()
         for i, t in enumerate((dq, dk, dv)):
             weight_grad(t, n1.at[l], gatt.at[0], 192, 192 * i)
         weight_grad(o.at[l], low, gatt.at[0], 192, 576)
+        finish(att_sum)
+        att_sum = all_sum(gatt, att_out.at[l], 1, core_a, half_a, full_a, sub_a, (sa_s, sa_r, ka_s))
+        running.append(att_sum)
+        tick()
         dx, gg, bg = norm_back(rs_done(), xs[...] if l == 1 else x0(me, mine), g_of(l, 0))
         vec_add(l, 0, gg, bg)
         g = carry[...] + dx
         carry[...] = g
         if l == 1:
             ag_send(g.astype(BF16).astype(F32))
+            tick()
     ag_send(carry[...])
+    running.append(sum_vecs())
+    tick()
 
     def grad_block(b, r):
-        tg_ref[r] = ag[r]
+        g = ag[r]
+        tg_ref[r] = g
+        for i in range(2):
+            sums_all[z, y, core, pl.ds(2 * b + i, 1), :] = jnp.sum(g[SEQ_LEN * i:SEQ_LEN * (i + 1)], axis=0, keepdims=True)
     ag_take(grad_block)
-
+    running.append(spread(sums_all, (st_s, st_r)))
+    tick()
     rs_send(lambda r, c: nn(act[1, r], wdown_ref[1, :, cols(c)]))
+    tick()
     ag_send((rs_done() + hs[1]).astype(BF16).astype(F32))
+    tick()
 
     def out_block(b, r):
         lo_ref[r] = ag[r].astype(BF16)
     ag_take(out_block)
+    tick()
+    tick()
+    table_sums()
+    while running:
+        tick()
 
 
 def on_device(nz, ny, nx, tokens, cotangent, buckets, time_table, w_qkv, w_out, w_up, w_down, norm_gain, norm_bias):
     trow = jnp.take(time_table, buckets, axis=0).astype(F32).reshape(-1, 1, D)
+    ids = jnp.broadcast_to(buckets[:, None], (buckets.shape[0], BLK))
     wqkv = w_qkv.transpose(0, 2, 3, 1).reshape(2, -1, D)
     vm = pl.BlockSpec(memory_space=pltpu.VMEM)
+    hbm = pl.BlockSpec(memory_space=pl.ANY)
     sd = jax.ShapeDtypeStruct
     sem = pltpu.SemaphoreType.DMA
-    out = pl.pallas_call(
+
+    def sum_bufs(n):
+        return [
+            pltpu.VMEM((n, 384, D), F32),
+            pltpu.VMEM((2, 2, n, 48, 384), F32),
+            pltpu.VMEM((2, 2, n, 96, 384), F32),
+            pltpu.VMEM((2, 3, n, 24, 384), F32),
+        ]
+
+    lo, tg, table, gain, bias, att, mlp = pl.pallas_call(
         functools.partial(body, nz, ny, nx),
-        out_shape=(sd((ROWS, D), BF16), sd((ROWS, D), F32), sd((2, D, D), F32), sd((1, D, D), F32),
-                   sd((2, D, D), F32), sd((1, D, D), F32), sd((8, D), F32)),
-        in_specs=[vm] * 9,
-        out_specs=(vm,) * 7,
+        out_shape=(sd((ROWS, D), BF16), sd((ROWS, D), F32), sd((192, time_table.shape[0]), F32),
+                   sd((2, 2, D), F32), sd((2, 2, D), F32),
+                   sd((2, 1, D, D), F32), sd((2, 2, D, D), F32)),
+        in_specs=[vm] * 10,
+        out_specs=(vm,) * 5 + (hbm,) * 2,
         scratch_shapes=[
+            pltpu.VMEM((2, D, D), F32),
+            pltpu.VMEM((1, D, D), F32),
+            pltpu.VMEM((2, D, D), F32),
+            pltpu.VMEM((1, D, D), F32),
+            pltpu.VMEM((8, D), F32),
             pltpu.VMEM((ROWS, D), F32),
             pltpu.VMEM((4, BLK, D), F32),
             pltpu.VMEM((2, HALF, D), F32),
@@ -385,27 +660,18 @@
             pltpu.VMEM((ROWS, 192), BF16),
             pltpu.VMEM((ROWS, 192), BF16),
             pltpu.VMEM((ROWS, 192), BF16),
-            sem((6,)), sem((6,)), sem((6,)), sem((6,)),
+        ] + sum_bufs(2) + sum_bufs(1) + [
+            pltpu.VMEM((4, 4, 8, D), F32),
+            pltpu.VMEM((4, 4, 2, 8, BLK), F32),
+            pltpu.VMEM((4, 4, 2, 8, D), F32),
+            sem((6,)), sem((6,)), sem((6,)), sem((6,)), sem((38,)), sem((38,)), sem((38,)), sem((38,)),
+            sem((10,)), sem((10,)), sem((7,)), sem((7,)), sem((7,)), sem((7,)), sem((2,)), sem((2,)),
         ],
-        compiler_params=pltpu.CompilerParams(collective_id=0, has_side_effects=True, vmem_limit_bytes=60 * 2 ** 20),
+        compiler_params=pltpu.CompilerParams(collective_id=0, has_side_effects=True, vmem_limit_bytes=62 * 2 ** 20),
         name="layers",
-    )(tokens, trow, cotangent, wqkv, w_out, w_up, w_down, norm_gain.reshape(4, D), norm_bias.reshape(4, D))
-    lo, tg, gm1, ga1, gm0, ga0, vec = out
-    mats = jnp.concatenate([ga0, gm0, ga1, gm1])
-    mats = lax.psum(mats, "dp")
-    vec = lax.psum(vec, ("dp", "tensor"))
-    col = lax.axis_index("tensor") * 192
-    sums = jnp.sum(tg.reshape(-1, SEQ_LEN, D), axis=1)
-    sums = lax.dynamic_slice_in_dim(sums, col, 192, 1)
-    sums = lax.all_gather(sums, "dp", axis=0, tiled=True)
-    ids = lax.all_gather(buckets, "dp", axis=0, tiled=True)
-    onehot = (ids[:, None] == jnp.arange(time_table.shape[0], dtype=jnp.int32)[None, :]).astype(F32)
-    table = jnp.einsum("sb,sd->bd", onehot, sums, precision=lax.Precision.HIGHEST)
-    att = jnp.stack([mats[0], mats[3]])
-    up = jnp.stack([mats[1], mats[4]])
-    down = jnp.stack([mats[2], mats[5]])
-    qkv = att[:, 0:576].reshape(2, 3, 192, D).transpose(0, 3, 1, 2)
-    return (lo, tg, table, qkv, att[:, 576:768], up, down, vec[0:4].reshape(2, 2, D), vec[4:8].reshape(2, 2, D))
+    )(tokens, trow, cotangent, ids, wqkv, w_out, w_up, w_down, norm_gain, norm_bias)
+    qkv = att[:, 0, 0:576].reshape(2, 3, 192, D).transpose(0, 3, 1, 2)
+    return (lo, tg, table.T, qkv, att[:, 0, 576:768], mlp[:, 0], mlp[:, 1], gain, bias)
 
 
 def solution(mesh):

time: 443 us -> 284 us (0.64)
  blocking collectives: 118 us -> 0 us
  waiting for transfers between devices: 30.1 us -> 0 us
  Pallas kernels: 235 us -> 261 us
  other arithmetic: 21.6 us -> 2.03 us
  between operations: 14.8 us -> 0.67 us
    psum x1 -> x0, blocking collectives: 79.3 us -> none  [on_device(): vec = lax.psum(vec, ('dp', 'tensor'))]
    psum x1 -> x0, waiting for transfers between devices: 30.1 us -> none  [on_device(): mats = lax.psum(mats, 'dp')]
    all_gather x1 -> x0, blocking collectives: 27.7 us -> none  [on_device(): sums = lax.all_gather(sums, 'dp', axis=0, tiled=True)]
    pallas_call x1, Pallas kernels: 235 us -> 261 us  [on_device(): pl.pallas_call(functools.partial(body, nz, ny, nx), out_shape=(sd((ROWS,...]
    unnamed x1 -> x0, blocking collectives: 11.1 us -> none
    concatenate x1 -> x0, other arithmetic: 10.5 us -> none  [on_device(): mats = jnp.concatenate([ga0, gm0, ga1, gm1])]
    another operation x3 -> x0, other arithmetic: 8.68 us -> none  [the longest x1 4.34 us: on_device(): up = jnp.stack([mats[1], mats[4]])]
    squeeze x0 -> x2, local copies, waits for them, and re-layouts: none -> 6.87 us  [the longest x1 4.36 us: on_device(): mlp[:, 1]]
  transfers between devices with their start and end apart: 1 -> 0, of which waited for: 1 -> 0; matrix products, arithmetic and copies ran while one was open for 1% -> 0% of each run, Pallas kernels for 0% -> 0%
where the time goes in v2:
time: 284 us
  Pallas kernels  261 us (92%)
  local copies, waits for them, and re-layouts  20.2 us (7%)
    pallas_call x1, Pallas kernels, on_device(): pl.pallas_call(functools.partial(body, nz, ny, nx), out_shape=(sd((ROWS,...  261 us

profile of v2, /device:TPU:1, one launch (start us, length us, event | category | flops | bytes accessed | tf_op | source)
XLA Modules:
  0.0 283.6 jit_solution(15797610011235227154)
XLA Ops:
  0.6 0.7 compare_and_fusion
  1.3 0.7 compare_select_fusion
  2.0 1.3 broadcast_in_dim.21.ids_ref
  3.3 2.8 %gather_fusion = bf16[8,768]{1,0:T(8,128)(2,1)S(1)} fusion(bf16[2000,768]{1,0:T(8,128)(2,1)} %param.13, s32[1024]{0:T(1024)S(1)} %pad_clamp_fusion), kind=kCustom, calls=%fused_computation | custom fusion | bytes 24608 | tf_op jit(solution)/shard_map/jit(_take)/gather | solution.py:613
  6.1 0.7 fusion.trow_ref
  6.8 260.7 %layers.1 = (bf16[512,768]{1,0:T(8,128)(2,1)}, f32[512,768]{1,0:T(8,128)}, f32[192,2000]{1,0:T(8,128)}, f32[2,2,768]{2,1,0:T(2,128)}, f32[2,2,768]{2,1,0:T(2,128...) custom-call(bf16[512,768]{1,0:T(8,128)(2,1)} %tok_ref.1, f32[8,1,768]{2,1,0:T(1,128)} %fusion.trow_ref, ...), custom_call_target="tpu_custom_call" | custom-call | tf_op jit(solution)/shard_map/layers/pallas_call | solution.py:629
  267.5 0.0 copy-start
  267.5 2.5 slice_bitcast_fusion.2
  270.0 4.8 %slice.12 = f32[2,1,576,768]{3,2,1,0:T(8,128)} slice(f32[2,1,768,768]{3,2,1,0:T(8,128)} %get-tuple-element.19), slice={[0:2], [0:1], [0:576], [0:768]} | slice | bytes 7077888 | tf_op jit(solution)/shard_map/slice | solution.py:673
  274.8 0.0 copy-done
  274.8 0.0 copy-start.3
  274.8 0.0 copy-start.2
  274.8 4.4 %slice_bitcast_fusion = (f32[2,768,768]{2,1,0:T(8,128)}, f32[2,768,768]{2,1,0:T(8,128)}) fusion(f32[2,2,768,768]{3,2,1,0:T(8,128)S(1)} %copy-done), kind=kLoop, calls=%fused_computation.1 | loop fusion | bytes 18874368 | tf_op jit(solution)/shard_map/squeeze | solution.py:674
  279.2 0.0 copy-start.1
  279.2 0.0 copy-done.3
  279.2 0.9 copy.28
  280.1 0.0 copy-done.2
  280.1 0.0 copy-start.5
  280.1 0.0 copy-start.4
  280.1 1.1 copy.29
  281.2 0.0 copy-done.1
  281.2 1.1 copy.30
  282.3 0.0 copy-done.5
  282.3 0.6 copy.31
  282.9 0.0 copy-done.4
  283.0 0.6 copy.32
  (1 shorter events, 0.0 us)
Async XLA Ops:
  267.5 7.3 %copy-start = (f32[2,2,768,768]{3,2,1,0:T(8,128)S(1)}, f32[2,2,768,768]{3,2,1,0:T(8,128)}, u32[]{:S(2)}) copy-start(f32[2,2,768,768]{3,2,1,0:T(8,128)} %get-tuple-element.20) | copy-start | bytes 28311556
  274.8 4.4 %copy-start.3 = (bf16[512,768]{1,0:T(8,128)(2,1)S(1)}, bf16[512,768]{1,0:T(8,128)(2,1)}, u32[]{:S(2)}) copy-start(bf16[512,768]{1,0:T(8,128)(2,1)} %get-tuple-element.34) | copy-start | bytes 2359300
  274.8 5.2 %copy-start.2 = (f32[512,768]{1,0:T(8,128)S(1)}, f32[512,768]{1,0:T(8,128)}, u32[]{:S(2)}) copy-start(f32[512,768]{1,0:T(8,128)} %get-tuple-element.35) | copy-start | bytes 4718596
  279.2 2.0 copy-start.1
  280.1 2.3 copy-start.5
  280.1 2.9 %copy-start.4 = (f32[2,2,768]{2,1,0:T(2,128)S(1)}, f32[2,2,768]{2,1,0:T(2,128)}, u32[]{:S(2)}) copy-start(f32[2,2,768]{2,1,0:T(2,128)} %get-tuple-element.42) | copy-start | bytes 36868

commit v3 on v1

v3 whole, which is shorter than its diff:
```python
import functools

import jax
import jax.numpy as jnp
from jax import lax
from jax.experimental import pallas as pl
from jax.experimental.pallas import tpu as pltpu
from jax.sharding import PartitionSpec as P

MESH = pl.DeviceIdType.MESH
F32 = jnp.float32
BF16 = jnp.bfloat16
HEAD_DIM = 64
SEQ_LEN = 64
D = 768
ROWS = 512
BLK = 128
HALF = 64
COLS = 256
EPS = 1e-05
GELU_A = 0.7978845608028654
GELU_B = 0.044715


def nn(a, b):
    return lax.dot_general(a, b, (((1,), (0,)), ((), ())), preferred_element_type=F32)


def nt(a, b):
    return lax.dot_general(a, b, (((1,), (1,)), ((), ())), preferred_element_type=F32)


def tn(a, b):
    return lax.dot_general(a, b, (((0,), (0,)), ((), ())), preferred_element_type=F32)


def norm_parts(x):
    c = x - jnp.mean(x, axis=-1, keepdims=True)
    r = lax.rsqrt(jnp.mean(c * c, axis=-1, keepdims=True) + EPS)
    return c * r, r


def norm(x, g, b):
    return norm_parts(x)[0] * g + b


def norm_back(dn, x, g):
    xh, r = norm_parts(x)
    dx = dn * g
    dx = r * (dx - jnp.mean(dx, axis=-1, keepdims=True) - xh * jnp.mean(dx * xh, axis=-1, keepdims=True))
    return dx, jnp.sum(dn * xh, axis=0, keepdims=True), jnp.sum(dn, axis=0, keepdims=True)


def gelu_cdf(u):
    t = jnp.tanh(GELU_A * (u + GELU_B * (u * u * u)))
    return t, 0.5 + 0.5 * t


def gelu(u):
    return u * gelu_cdf(u)[1]


def gelu_slope(u):
    t, cdf = gelu_cdf(u)
    return cdf + u * (0.5 * (1.0 - t * t)) * (GELU_A * (1.0 + 3.0 * GELU_B * (u * u)))


def body(nz, ny, nx,
         tok_ref, trow_ref, cot_ref, ids_ref, wqkv_ref, wout_ref, wup_ref, wdown_ref, gain_ref, bias_ref,
         lo_out, tg_out, table_out, gain_out, bias_out, att_out, mlp_out, land, core_m, core_a, n1_all, n2_all, da_all,
         gmat, gatt, vec_ref, ag, sbuf, rh, rf, n1, n2, act, q, k, v, o, u, prob, hs, xs, carry, gmlow, low, du, dq, dk, dv,
         watt, wst, acc, acc2, src_x, take_x,
         mine_w, far_w, stage, half_m, full_m, sub_m, half_a, full_a, sub_a, vecs, ids_all, sums_all,
         rs_s, rs_r, ag_s, ag_r, gx_s, gx_r, sm_s, sm_r, sa_s, sa_r, sw_s, sw_r, sv_s, sv_r, si_s, si_r, st_s, st_r,
         keep_s, stage_s, wst_s, take_s, out_s):
    dp = lax.axis_index("dp")
    me = lax.axis_index("tensor")
    core = lax.rem(dp, 2)
    y = lax.rem(dp // 2, ny)
    z = dp // (2 * ny)
    right = (dp, lax.rem(me + 1, nx))
    left = (dp, lax.rem(me + nx - 1, nx))

    def at(zz, yy, cc):
        return ((lax.rem(zz, nz) * ny + lax.rem(yy, ny)) * 2 + lax.rem(cc, 2), me)

    def along(axis, o):
        return at(z, y + o, core) if axis == 0 else at(z + o, y, core)

    twin = at(z, y, core + 1)

    bar = pltpu.get_barrier_semaphore()
    peers = [(dp, lax.rem(me + i, nx)) for i in (1, 2, 3)] + [along(a, i) for a in (0, 1) for i in (1, 2, 3)] + [twin]
    for peer in peers:
        pl.semaphore_signal(bar, inc=1, device_id=peer, device_id_type=MESH)
    pl.semaphore_wait(bar, len(peers))

    def rows(b):
        return pl.ds(pl.multiple_of(b * BLK, BLK), BLK)

    def half(b, i):
        return pl.ds(pl.multiple_of(b * BLK + i * HALF, HALF), HALF)

    def turn(rel):
        return lax.rem(me + rel, nx)

    mine = rows(me)

    now = [0.0]
    free = {"core": 0.0, "yz": 0.0, "x": 0.0}
    running = []

    def work(t):
        now[0] += t

    def link(which, t):
        free[which] = max(now[0], free[which]) + t
        return free[which] + 2.0

    def advance(entry):
        now[0] = max(now[0], entry[1])
        got = next(entry[0], None)
        if got is None:
            running.remove(entry)
        else:
            entry[1], entry[2] = got if isinstance(got, tuple) else (got, 0.3)

    def begin(gen):
        entry = [gen, 0.0, 0.0]
        running.append(entry)
        advance(entry)
        return entry

    def idle(until, late=0.5):
        while True:
            fit = [e for e in running if max(now[0], e[1]) + e[2] <= until + late]
            if not fit:
                break
            advance(min(fit, key=lambda e: (max(now[0], e[1]), e[2])))
        now[0] = max(now[0], until)

    def ready():
        idle(now[0])

    def finish(entry):
        while entry in running:
            advance(min(running, key=lambda e: e[1]))

    def after(which):
        while which not in sums or sums[which] in running:
            yield max(now[0], sums[which][1] if which in sums else 0.0) + 0.5, 0.0

    def rs_copy(i):
        src, dst, to = [
            (sbuf.at[0, 0:HALF], rh.at[0], right),
            (sbuf.at[0, HALF:BLK], rh.at[1], left),
            (sbuf.at[1, HALF:BLK], rf.at[0, HALF:BLK], right),
            (sbuf.at[2, 0:HALF], rf.at[1, 0:HALF], left),
            (sbuf.at[1, 0:HALF], rf.at[0, 0:HALF], right),
            (sbuf.at[2, HALF:BLK], rf.at[1, HALF:BLK], left),
        ][i]
        return pltpu.make_async_remote_copy(
            src_ref=src, dst_ref=dst, send_sem=rs_s.at[i], recv_sem=rs_r.at[i], device_id=to, device_id_type=MESH)

    rs_end = [0.0]

    def rs_send(part, cost):
        began = 0.0
        for j, rel in enumerate((2, 1, 3, 0)):
            r = rows(turn(rel))
            for c in range(D // COLS):
                sbuf[j, :, c * COLS:(c + 1) * COLS] = part(r, c)
            work(cost)
            if j == 0:
                rs_copy(0).start()
                rs_copy(1).start()
                began = link("x", 12.5) - 14.5
            if j == 1:
                rs_copy(2).start()
            if j == 2:
                rs_copy(3).start()
                idle(began + 6.0)
                rs_copy(0).wait_recv()
                sbuf[1, 0:HALF] += rh[0]
                rs_copy(4).start()
                rs_copy(1).wait_recv()
                sbuf[2, HALF:BLK] += rh[1]
                rs_copy(5).start()
                work(0.2)
        rs_end[0] = began + 14.0
        ready()

    def rs_done():
        idle(rs_end[0])
        for i in range(2, 6):
            rs_copy(i).wait_recv()
        total = sbuf[3] + rf[0] + rf[1]
        for i in range(6):
            rs_copy(i).wait_send()
        work(1.0)
        return total

    def ag_copy(i, arriving=False):
        if arriving:
            b, h = [(3, 0), (1, 1), (3, 1), (1, 0), (2, 0), (2, 1)][i]
        else:
            b, h = [(0, 0), (0, 1), (0, 1), (0, 0), (3, 0), (1, 1)][i]
        at = half(turn(b), h)
        return pltpu.make_async_remote_copy(
            src_ref=ag.at[at], dst_ref=ag.at[at], send_sem=ag_s.at[i], recv_sem=ag_r.at[i],
            device_id=[right, left][i % 2], device_id_type=MESH)

    ag_began = [0.0]

    def ag_send(val):
        ag[mine] = val
        for i in range(4):
            ag_copy(i).start()
        ag_began[0] = link("x", 12.5) - 14.5

    def ag_take(fn, cost):
        for j, rel in enumerate((0, 3, 1, 2)):
            blk = turn(rel)
            if j == 1:
                idle(ag_began[0] + 5.7)
                ag_copy(0, True).wait_recv()
                ag_copy(4).start()
                ag_copy(1, True).wait_recv()
                ag_copy(5).start()
                idle(ag_began[0] + 9.9)
                ag_copy(2, True).wait_recv()
            if j == 2:
                ag_copy(3, True).wait_recv()
            if j == 3:
                idle(ag_began[0] + 14.0)
                ag_copy(4, True).wait_recv()
                ag_copy(5, True).wait_recv()
            fn(blk, rows(blk))
            work(cost)
            ready()
        for i in range(6):
            ag_copy(i).wait_send()

    def each(fn, cost):
        def step(j, _):
            fn(j, rows(j))
            return 0
        lax.fori_loop(0, nx // 2, step, 0)
        work(2 * cost)
        ready()
        lax.fori_loop(nx // 2, nx, step, 0)
        work(2 * cost)
        ready()

    def gather_x(w, dst):
        src = src_x.at[w]

        def copy(i, arriving=False):
            if arriving:
                b, h = [(3, 0), (1, 1), (3, 1), (1, 0), (2, 0), (2, 1)][i]
            else:
                b, h = [(0, 0), (0, 1), (0, 1), (0, 0), (3, 0), (1, 1)][i]
            to = dst.at[half(turn(b), h)]
            fr = to if arriving or i > 3 else src.at[h * HALF:(h + 1) * HALF]
            return pltpu.make_async_remote_copy(
                src_ref=fr, dst_ref=to, send_sem=gx_s.at[w, i], recv_sem=gx_r.at[w, i],
                device_id=[right, left][i % 2], device_id_type=MESH)

        for i in range(4):
            copy(i).start()
        keep = pltpu.make_async_copy(src, dst.at[mine], keep_s.at[5 + w])
        keep.start()
        first = link("x", 4.2)
        link("x", 4.2)
        yield first
        copy(0, True).wait_recv()
        copy(4).start()
        copy(1, True).wait_recv()
        copy(5).start()
        yield link("x", 4.2)
        for i in range(2, 6):
            copy(i, True).wait_recv()
        for i in range(6):
            copy(i).wait_send()
        keep.wait()

    def taken(from_ref, fn, cost):
        def fetch(b):
            return pltpu.make_async_copy(from_ref.at[b * BLK:(b + 1) * BLK], take_x.at[b % 2], take_s.at[b % 2])
        fetch(0).start()
        for b in range(4):
            if b < 3:
                fetch(b + 1).start()
            yield now[0], cost
            fetch(b).wait()
            fn(b, slice(b * BLK, (b + 1) * BLK), take_x[b % 2].astype(BF16))
            work(cost)

    def g_of(l, i):
        return gain_ref[l, i:i + 1, :]

    def b_of(l, i):
        return bias_ref[l, i:i + 1, :]

    def x0(b, r):
        x = tok_ref[r].astype(F32)
        s = lax.broadcasted_iota(jnp.int32, (BLK, 1), 0) < SEQ_LEN
        return x + jnp.where(s, trow_ref[2 * b], trow_ref[2 * b + 1])

    iq = lax.broadcasted_iota(jnp.int32, (BLK, BLK), 0) // SEQ_LEN
    ik = lax.broadcasted_iota(jnp.int32, (BLK, BLK), 1) // SEQ_LEN
    same = iq == ik
    lane = lax.broadcasted_iota(jnp.int32, (1, BLK), 1) // HEAD_DIM
    heads = [(slice(0, 128), (lane == 0).astype(F32).astype(BF16)), (slice(0, 128), (lane == 1).astype(F32).astype(BF16)),
             (slice(128, 192), None)]

    def only(x, m):
        return x if m is None else x * m

    def attn_out(qr, kr, vr, o_, pr):
        outs = []
        for i, (c, m) in enumerate(heads):
            s = nt(only(qr[:, c], m), kr[:, c]) * HEAD_DIM ** -0.5
            s = jnp.where(same, s, -1e30)
            e = jnp.exp(s - jnp.max(s, axis=-1, keepdims=True))
            p = e / jnp.sum(e, axis=-1, keepdims=True)
            pr[i] = p
            outs.append(nn(p.astype(BF16), only(vr[:, c], m)))
        o_[:, 0:128] = (outs[0] + outs[1]).astype(BF16)
        o_[:, 128:192] = outs[2].astype(BF16)

    def qkv_attn(l, b, r, n):
        n1[l, r] = n
        for i, t in enumerate((q, k, v)):
            t[l, r, :] = nt(n, wqkv_ref[l, 192 * i:192 * (i + 1), :]).astype(BF16)
        attn_out(q.at[l, r], k.at[l, r], v.at[l, r], o.at[l, r], prob.at[l, pl.ds(3 * b, 3)])

    def qkv_attn_back(l, b, r, dl):
        low[l, r] = dl
        do = nt(dl, wout_ref[l]).astype(BF16)
        attn_back(q.at[l, r], k.at[l, r], v.at[l, r], prob.at[l, pl.ds(3 * b, 3)], do, dq.at[l, r], dk.at[l, r], dv.at[l, r])

    def attn_back(qr, kr, vr, pr, do, dqr, dkr, dvr):
        got = []
        for i, (c, m) in enumerate(heads):
            p = pr[i]
            pb = p.astype(BF16)
            d = only(do[:, c], m)
            dp_ = nt(d, vr[:, c])
            ds = (p * (dp_ - jnp.sum(p * dp_, axis=-1, keepdims=True))).astype(BF16)
            got.append((nn(ds, only(kr[:, c], m)), tn(ds, only(qr[:, c], m)), tn(pb, d)))
        for t, j, s in ((dqr, 0, HEAD_DIM ** -0.5), (dkr, 1, HEAD_DIM ** -0.5), (dvr, 2, 1.0)):
            t[:, 0:128] = ((got[0][j] + got[1][j]) * s).astype(BF16)
            t[:, 128:192] = (got[2][j] * s).astype(BF16)

    def mlp_up(r, n):
        n2[0, r] = n
        for c in range(D // COLS):
            cs = slice(c * COLS, (c + 1) * COLS)
            up = nn(n, wup_ref[0, :, cs])
            u[r, cs] = up
            act[0, r, cs] = gelu(up).astype(BF16)

    def mlp_back(r, gl):
        for c in range(D // COLS):
            cs = slice(c * COLS, (c + 1) * COLS)
            da = nt(gl, wdown_ref[0, cs, :])
            du[0, r, cs] = (da * gelu_slope(u[r, cs])).astype(BF16)

    def mlp_both(n, gl, wu, wd, a_, d_):
        for c in range(D // COLS):
            cs = slice(c * COLS, (c + 1) * COLS)
            up = nn(n, wu[:, cs])
            t, cdf = gelu_cdf(up)
            a_[:, cs] = (up * cdf).astype(BF16)
            slope = cdf + up * (0.5 * (1.0 - t * t)) * (GELU_A * (1.0 + 3.0 * GELU_B * (up * up)))
            d_[:, cs] = (nt(gl, wd[cs, :]) * slope).astype(BF16)

    def weight_grad(a, b, out, at=0):
        for c in range(D // COLS):
            cs = slice(c * COLS, (c + 1) * COLS)
            out[at:at + 192, cs] = tn(a[:, 0:192], b[:, cs])

    def weight_grad_wide(a, b, out):
        def step(i, _):
            at = pl.ds(pl.multiple_of(i * COLS, COLS), COLS)
            for c in range(D // COLS):
                cs = slice(c * COLS, (c + 1) * COLS)
                out[at, cs] = tn(a[:, at], b[:, cs])
            return 0
        lax.fori_loop(0, D // COLS, step, 0)
        work(1.5)

    def cols(c):
        return slice(c * COLS, (c + 1) * COLS)

    def vec_add(l, i, gg, bg):
        vec_ref[2 * l + i:2 * l + i + 1, :] = gg
        vec_ref[4 + 2 * l + i:5 + 2 * l + i, :] = bg

    def remote(src, dst, sems, i, to):
        return pltpu.make_async_remote_copy(
            src_ref=src, dst_ref=dst, send_sem=sems[0].at[i], recv_sem=sems[1].at[i], device_id=to, device_id_type=MESH)

    def shift1(o_):
        return at(z + core * o_, y + (1 - core) * o_, core)

    def shift2(o_):
        return at(z + (1 - core) * o_, y + core * o_, core)

    pos1 = y + core * (z - y)
    pos2 = z + core * (y - z)
    half_cols = pl.ds(pl.multiple_of(core * 384, 128), 384)
    twin_cols = pl.ds(pl.multiple_of((1 - core) * 384, 128), 384)

    def blk(o_, h=0):
        return lax.rem(pos1 + o_, 4) * 192 + h * 96

    def sub(o_):
        return blk(0) + lax.rem(pos2 + o_, 4) * 48

    def part(of, row, count, cs=half_cols):
        return of.at[:, pl.ds(pl.multiple_of(row, 16), count), cs]

    def add_into(mat, n, row, count, srcs, unit=96):
        unit = min(unit, count)

        def step(i, _):
            for kk in range(n):
                to = pl.ds(pl.multiple_of(row + i * unit, 16), unit)
                fr = pl.ds(pl.multiple_of(i * unit, 16), unit)
                val = mat[kk, to, half_cols]
                for src in srcs:
                    val = val + src[kk, fr, :]
                mat[kk, to, half_cols] = val
            return 0
        if count == unit:
            step(0, 0)
        else:
            lax.fori_loop(0, count // unit, step, 0)

    def add_core(mat, n, core_b):
        def fetch(i):
            kk, j = i // 4, i % 4
            return pltpu.make_async_copy(core_b.at[kk, pl.ds(192 * j, 192)], stage.at[i % 2], stage_s.at[i % 2])
        for i in range(2):
            fetch(i).start()
        for i in range(4 * n):
            fetch(i).wait()
            kk, j = i // 4, i % 4
            mat[kk, 192 * j:192 * (j + 1), half_cols] += stage[i % 2]
            if i + 2 < 4 * n:
                fetch(i + 2).start()
        work(0.5 + 0.8 * n)

    def hand_out(src, res, n, sems, keep_s):
        def copy(i):
            if i < 3:
                return remote(src, part(res, sub(0), 48), sems, i, shift2(i + 1))
            b, h, to = [(0, 0, 1), (0, 1, 3), (0, 1, 1), (0, 0, 3), (3, 0, 1), (1, 1, 3)][i - 3]
            ref = part(res, blk(b, h), 96)
            return remote(ref, ref, sems, i, shift1(to))

        def landing(i):
            if i < 3:
                ref = part(res, sub(3 - i), 48)
            else:
                b, h = [(3, 0), (1, 1), (3, 1), (1, 0), (2, 0), (2, 1)][i - 3]
                ref = part(res, blk(b, h), 96)
            return remote(ref, ref, sems, i, twin)

        for i in range(3):
            copy(i).start()
        keep = pltpu.make_async_copy(src, part(res, sub(0), 48), keep_s)
        keep.start()
        yield link("yz", 1.6 * n)
        keep.wait()
        for i in range(3):
            landing(i).wait_recv()
        for i in range(3, 7):
            copy(i).start()
        arrive = link("yz", 1.6 * n)
        link("yz", 1.6 * n)
        yield arrive
        landing(3).wait_recv()
        copy(7).start()
        landing(4).wait_recv()
        copy(8).start()
        yield link("yz", 1.6 * n)
        for i in range(5, 9):
            landing(i).wait_recv()
        last = remote(part(res, 0, D), part(res, 0, D), sems, 9, twin)
        last.start()
        for i in range(9):
            copy(i).wait_send()
        yield link("core", 2.0 * n)
        remote(part(res, 0, D, twin_cols), part(res, 0, D, twin_cols), sems, 9, twin).wait_recv()
        last.wait_send()

    def all_sum(mat, res, n, core_b, half_b, full_b, sub_b, sems, keep_s):
        def copy(i):
            if i < 6:
                src, dst, to = [
                    (part(mat, blk(2, 0), 96), half_b.at[0], 1),
                    (part(mat, blk(2, 1), 96), half_b.at[1], 3),
                    (part(mat, blk(1, 1), 96), full_b.at[0, :, 96:192], 1),
                    (part(mat, blk(3, 0), 96), full_b.at[1, :, 0:96], 3),
                    (part(mat, blk(1, 0), 96), full_b.at[0, :, 0:96], 1),
                    (part(mat, blk(3, 1), 96), full_b.at[1, :, 96:192], 3),
                ][i]
                return remote(src, dst, sems, 10 + i, shift1(to))
            o_ = i - 5
            return remote(part(mat, sub(o_), 48), sub_b.at[o_ - 1], sems, 10 + i, shift2(o_))

        c0 = remote(part(mat, 0, D, twin_cols), core_b, sems, 19, twin)
        c0.start()
        yield link("core", 2.0 * n)
        c0.wait_recv()
        add_core(mat, n, core_b)
        for i in range(4):
            copy(i).start()
        arrive = link("yz", 1.6 * n)
        link("yz", 1.6 * n)
        yield arrive
        copy(0).wait_recv()
        add_into(mat, n, blk(1, 0), 96, [half_b.at[0]])
        copy(4).start()
        copy(1).wait_recv()
        add_into(mat, n, blk(3, 1), 96, [half_b.at[1]])
        copy(5).start()
        work(0.3 * n)
        yield link("yz", 1.6 * n)
        for i in (2, 3, 4, 5):
            copy(i).wait_recv()
        add_into(mat, n, blk(0), 192, [full_b.at[0], full_b.at[1]])
        for i in (6, 7, 8):
            copy(i).start()
        c0.wait_send()
        work(0.5 * n)
        yield link("yz", 1.6 * n)
        for i in (6, 7, 8):
            copy(i).wait_recv()
        add_into(mat, n, sub(0), 48, [sub_b.at[0], sub_b.at[1], sub_b.at[2]])
        for i in range(9):
            copy(i).wait_send()
        work(0.2 * n)
        yield from hand_out(part(mat, sub(0), 48), res, n, sems, keep_s)

    released = [0]

    def fetch_weights(m, fill, use):
        own = mine_w.at[m]
        sems, keep_ = (sw_s.at[m], sw_r.at[m]), keep_s.at[m]
        fill(own)
        sent = [remote(own, far_w.at[m, pl.ds(3 - i, 1)], sems, 9 + i, (dp, lax.rem(me + i, nx))) for i in (1, 2, 3)]
        for cp in sent:
            cp.start()
        yield link("x", 3.2)
        while m > released[0]:
            yield now[0] + 1.0, 0.0
        for cp in sent:
            cp.wait_recv()
        yield from hand_out(far_w.at[m], land.at[m], 3, sems, keep_)
        for cp in sent:
            cp.wait_send()
        use()

    def spread(buf, sems):
        def group(i):
            if i < 3:
                return buf.at[z, y, core], along(1, i + 1), lambda: buf.at[lax.rem(z + 3 - i, 4), y, core]
            if i < 6:
                return buf.at[:, y, core], along(0, i - 2), lambda: buf.at[:, lax.rem(y + 6 - i, 4), core]
            return buf.at[:, :, core], twin, lambda: buf.at[:, :, lax.rem(core + 1, 2)]

        for some in ((0, 1, 2), (3, 4, 5), (6,)):
            for i in some:
                src, to, _ = group(i)
                remote(src, src, sems, i, to).start()
            yield now[0] + 5.0
            for i in some:
                src, to, where = group(i)
                remote(where(), where(), sems, i, to).wait_recv()
            for i in some:
                src, to, _ = group(i)
                remote(src, src, sems, i, to).wait_send()

    def sum_vecs():
        val = vec_ref[...]
        i = 0
        for stage, (pos, peers_) in enumerate((
                (me, [(dp, lax.rem(me + i_, nx)) for i_ in (1, 2, 3)]),
                (z, [along(1, i_) for i_ in (1, 2, 3)]),
                (y, [along(0, i_) for i_ in (1, 2, 3)]),
                (core, [twin]))):
            count = len(peers_) + 1
            buf = vecs.at[stage]
            buf[pos] = val
            sent = []
            for j, to in enumerate(peers_):
                cp = remote(buf.at[pos], buf.at[pos], (sv_s, sv_r), i + j, to)
                cp.start()
                sent.append(cp)
            yield now[0] + 4.0
            for j in range(len(peers_)):
                ref = buf.at[lax.rem(pos + count - 1 - j, count)]
                remote(ref, ref, (sv_s, sv_r), i + j, twin).wait_recv()
            for cp in sent:
                cp.wait_send()
            i += len(peers_)
            val = buf[0]
            for j in range(1, count):
                val = val + buf[j]
        for l in range(2):
            for w in range(2):
                gain_out[l, w:w + 1, :] = val[2 * l + w:2 * l + w + 1, :]
                bias_out[l, w:w + 1, :] = val[4 + 2 * l + w:5 + 2 * l + w, :]

    def table_sums():
        ids = ids_all[...].reshape(256, BLK)[:, 0:1]
        rest = sums_all[...].reshape(256, 256)[:, 0:192]
        parts = []
        for _ in range(3):
            top = rest.astype(BF16)
            parts.append(top)
            rest = rest - top.astype(F32)
        out = []
        for i in range(4):
            hot = lax.broadcasted_iota(jnp.int32, (256, 512), 1).astype(F32) + float(512 * i) == ids
            hot = hot.astype(F32).astype(BF16)
            to = ag.at[0:192, 0:512] if i % 2 == 0 else ag.at[192:384, 0:512]
            if i > 1:
                out[i - 2].wait()
            to[...] = tn(parts[0], hot) + (tn(parts[1], hot) + tn(parts[2], hot))
            cp = pltpu.make_async_copy(to, table_out.at[:, 512 * i:512 * (i + 1)], out_s.at[i])
            cp.start()
            out.append(cp)
        out[2].wait()
        out[3].wait()

    sums = {}

    ids_all[z, y, core] = ids_ref[...].astype(F32)
    begin(spread(ids_all, (si_s, si_r)))
    w_row = pl.multiple_of(sub(0), 16)

    def fill_att(ref):
        @pl.when(w_row < 576)
        def _():
            ref[0] = wqkv_ref[1, pl.ds(w_row, 48), half_cols].astype(F32)

        @pl.when(w_row >= 576)
        def _():
            ref[0] = wout_ref[1, pl.ds(w_row - 576, 48), half_cols].astype(F32)

    def fill_up(ref):
        ref[0] = wup_ref[1, pl.ds(w_row, 48), half_cols].astype(F32)

    def fill_down(ref):
        ref[0] = wdown_ref[1, pl.ds(w_row, 48), half_cols].astype(F32)

    def use_att():
        def fetch(i):
            j, h = i // 2, i % 2
            return pltpu.make_async_copy(land.at[0, j, pl.ds(384 * h, 384)], gmat.at[i % 2, 0:384], wst_s.at[i % 2])
        fetch(0).start()
        for i in range(6):
            if i < 5:
                fetch(i + 1).start()
            fetch(i).wait()
            j, h = i // 2, i % 2
            watt[j, 384 * h:384 * (h + 1)] = gmat[i % 2, 0:384].astype(BF16)
        work(4.0)
    att_weights = begin(fetch_weights(0, fill_att, use_att))
    up_weights = begin(fetch_weights(1, fill_up, lambda: None))
    down_weights = begin(fetch_weights(2, fill_down, lambda: None))

    def first(b, r):
        qkv_attn(0, b, r, norm(x0(b, r), g_of(0, 0), b_of(0, 0)).astype(BF16))
    each(first, 2.2)
    rs_send(lambda r, c: nn(o[0, r], wout_ref[0, :, cols(c)]), 0.4)
    released[0] = 1
    h = rs_done() + x0(me, mine)
    hs[0] = h
    ag_send(norm(h, g_of(0, 1), b_of(0, 1)).astype(BF16).astype(F32))

    def up_block(b, r):
        mlp_up(r, ag[r].astype(BF16))
    ag_take(up_block, 1.0)
    released[0] = 2
    rs_send(lambda r, c: nn(act[0, r], wdown_ref[0, :, cols(c)]), 0.7)
    x1 = rs_done() + hs[0]
    xs[...] = x1

    n1d, lowd, ad, dud = (t.at[1, 0:BLK] for t in (n1, low, act, du))
    dqd, dkd, dvd = (t.at[1, 0:BLK] for t in (dq, dk, dv))

    def shard(t, j):
        return t.at[1, rows(j)]

    def shard_prob(j):
        return prob.at[1, pl.ds(3 * j, 3)]

    n = norm(x1, g_of(1, 0), b_of(1, 0)).astype(BF16)
    n1d[...] = n
    src_x[0] = n.astype(F32)
    sums["n1"] = begin(gather_x(0, n1_all))
    finish(att_weights)

    def local_attn(j, wq, wo):
        for i, t in enumerate((q, k, v)):
            shard(t, j)[...] = nt(n1d[...], wq[192 * i:192 * (i + 1), :]).astype(BF16)
        attn_out(shard(q, j), shard(k, j), shard(v, j), shard(o, j), shard_prob(j))
        for c in range(D // COLS):
            acc[:, cols(c)] += nn(shard(o, j)[...], wo[:, cols(c)])

    def others(fn):
        def step(j, _):
            fn(j + 1, watt.at[j, 0:576], watt.at[j, 576:768])
            return 0
        lax.fori_loop(0, nx - 1, step, 0)

    acc[...] = x1
    local_attn(0, wqkv_ref.at[1], wout_ref.at[1])
    others(local_attn)
    work(7.0)
    ready()
    h = acc[...]
    hs[1] = h
    n = norm(h, g_of(1, 1), b_of(1, 1)).astype(BF16)
    lowd[...] = n
    src_x[1] = n.astype(F32)
    sums["n2"] = begin(gather_x(1, n2_all))
    finish(up_weights)
    finish(down_weights)

    def fetch_mlp(j, w):
        return pltpu.make_async_copy(land.at[1 + w, j], gmat.at[w], wst_s.at[w])

    acc2[...] = jnp.zeros_like(acc2)
    cot_own = cot_ref[mine]
    for w in range(2):
        fetch_mlp(0, w).start()
    for j in range(nx):
        if j == 0:
            wu, wd = wup_ref.at[1], wdown_ref.at[1]
        else:
            wu, wd = wst.at[0], wst.at[1]
            for w in range(2):
                fetch_mlp(j - 1, w).wait()
                wst[w] = gmat[w].astype(BF16)
                if j < nx - 1:
                    fetch_mlp(j, w).start()
        mlp_both(lowd[...], cot_own, wu, wd, ad, dud)
        for c in range(D // COLS):
            acc[:, cols(c)] += nn(ad[...], wd[:, cols(c)])
            acc2[:, cols(c)] += nt(dud[...], wu[cols(c), :])
        work(4.0)
        ready()
    src_x[3] = acc[...].astype(BF16).astype(F32)
    dx, gg, bg = norm_back(acc2[...], hs[1], g_of(1, 1))
    vec_add(1, 1, gg, bg)
    dh = cot_own.astype(F32) + dx
    carry[...] = dh
    lowd[...] = dh.astype(BF16)
    src_x[2] = lowd[...].astype(F32)
    acc[...] = jnp.zeros_like(acc)

    def local_attn_back(j, wq, wo):
        do = nt(lowd[...], wo[...]).astype(BF16)
        attn_back(shard(q, j), shard(k, j), shard(v, j), shard_prob(j), do, dqd, dkd, dvd)
        for c in range(D // COLS):
            acc[:, cols(c)] += (nn(dqd[...], wq[0:192, cols(c)]) + nn(dkd[...], wq[192:384, cols(c)])
                                + nn(dvd[...], wq[384:576, cols(c)]))
    local_attn_back(0, wqkv_ref.at[1], wout_ref.at[1])
    others(local_attn_back)
    work(7.0)
    ready()
    dx, gg, bg = norm_back(acc[...], xs[...], g_of(1, 0))
    vec_add(1, 0, gg, bg)
    g = carry[...] + dx
    carry[...] = g
    ag_send(g.astype(BF16).astype(F32))

    def mlp_grads(l, glow, then):
        yield now[0], 1.5
        weight_grad_wide(act.at[l], glow, gmat.at[2 * l + 1])
        yield now[0], 1.5
        weight_grad_wide(n2.at[l], du.at[l], gmat.at[2 * l])
        sums["mlp", l] = begin(all_sum(gmat.at[2 * l:2 * l + 2], mlp_out.at[:, l], 2, core_m.at[l], half_m.at[l], full_m.at[l], sub_m.at[l],
                                       (sm_s.at[l], sm_r.at[l]), keep_s.at[3 + l]))

    def att_grads(l):
        for i, t in enumerate((dq, dk, dv)):
            weight_grad(t.at[l], n1.at[l], gatt.at[l, 0], 192 * i)
        weight_grad(o.at[l], low.at[l], gatt.at[l, 0], 576)
        work(1.5)
        sums["att", l] = begin(all_sum(gatt.at[l], att_out.at[l], 1, core_a.at[l], half_a.at[l], full_a.at[l], sub_a.at[l],
                                       (sa_s.at[l], sa_r.at[l]), keep_s.at[9 + l]))

    def layer1_grads():
        yield from after("n2")

        def both(b, r, n):
            n2[1, r] = n
            mlp_both(n, cot_ref[r], wup_ref.at[1], wdown_ref.at[1], act.at[1, r], du.at[1, r])
        yield from taken(n2_all, both, 2.0)
        yield from mlp_grads(1, cot_ref, None)
        yield from after("n1")
        yield from taken(n1_all, lambda b, r, n: qkv_attn(1, b, r, n), 2.0)
        yield from after("dha")
        yield from taken(da_all, lambda b, r, n: qkv_attn_back(1, b, r, n), 1.7)
        yield now[0], 1.5
        att_grads(1)
    grads1 = begin(layer1_grads())

    def back_block(b, r):
        gl = ag[r].astype(BF16)
        gmlow[r] = gl
        mlp_back(r, gl)
    ag_take(back_block, 0.8)
    rs_send(lambda r, c: nt(du[0, r], wup_ref[0, cols(c), :]), 0.7)
    sums["dha"] = begin(gather_x(2, da_all))
    grads0 = begin(mlp_grads(0, gmlow, None))
    dx, gg, bg = norm_back(rs_done(), hs[0], g_of(0, 1))
    vec_add(0, 1, gg, bg)
    dh = carry[...] + dx
    carry[...] = dh
    ag_send(dh.astype(BF16).astype(F32))
    ag_take(lambda b, r: qkv_attn_back(0, b, r, ag[r].astype(BF16)), 1.5)
    att_grads(0)
    rs_send(lambda r, c: nn(dq[0, r], wqkv_ref[0, 0:192, cols(c)]) + nn(dk[0, r], wqkv_ref[0, 192:384, cols(c)])
            + nn(dv[0, r], wqkv_ref[0, 384:576, cols(c)]), 0.7)
    dx, gg, bg = norm_back(rs_done(), x0(me, mine), g_of(0, 0))
    vec_add(0, 0, gg, bg)
    ag_send(carry[...] + dx)
    begin(sum_vecs())
    begin(gather_x(3, lo_out))

    def grad_block(b, r):
        g = ag[r]
        for i in range(2):
            total = jnp.sum(g[SEQ_LEN * i:SEQ_LEN * (i + 1)], axis=0, keepdims=True)
            own = total[:, 0:192]
            for t in range(1, 4):
                own = jnp.where(me == t, total[:, 192 * t:192 * (t + 1)], own)
            sums_all[z, y, core, pl.ds(2 * b + i, 1), 0:192] = own
    ag_take(grad_block, 0.3)
    spreading = begin(spread(sums_all, (st_s, st_r)))
    tg_copy = pltpu.make_async_copy(ag, tg_out, out_s.at[4])
    tg_copy.start()
    finish(spreading)
    tg_copy.wait()
    table_sums()
    work(1.0)
    while running:
        advance(min(running, key=lambda e: e[1]))


def on_device(nz, ny, nx, tokens, cotangent, buckets, time_table, w_qkv, w_out, w_up, w_down, norm_gain, norm_bias):
    trow = jnp.take(time_table, buckets, axis=0).astype(F32).reshape(-1, 1, D)
    ids = jnp.broadcast_to(buckets[:, None], (buckets.shape[0], BLK))
    wqkv = w_qkv.transpose(0, 2, 3, 1).reshape(2, -1, D)
    vm = pl.BlockSpec(memory_space=pltpu.VMEM)
    hbm = pl.BlockSpec(memory_space=pl.ANY)
    sd = jax.ShapeDtypeStruct
    sem = pltpu.SemaphoreType.DMA

    def sum_bufs(n):
        return [
            pltpu.VMEM((2, 2, n, 96, 384), F32),
            pltpu.VMEM((2, 2, n, 192, 384), F32),
            pltpu.VMEM((2, 3, n, 48, 384), F32),
        ]

    def sems(*n):
        return [sem(n), sem(n)]

    lo, tg, table, gain, bias, att, mlp = pl.pallas_call(
        functools.partial(body, nz, ny, nx),
        out_shape=(sd((ROWS, D), F32), sd((ROWS, D), F32), sd((192, 2048), F32), sd((2, 2, D), F32), sd((2, 2, D), F32),
                   sd((2, 1, D, D), F32), sd((2, 2, D, D), F32),
                   sd((3, 3, D, D), F32), sd((2, 2, D, 384), F32), sd((2, 1, D, 384), F32),
                   sd((ROWS, D), F32), sd((ROWS, D), F32), sd((ROWS, D), F32)),
        in_specs=[vm] * 10,
        out_specs=(hbm, hbm, hbm, vm, vm) + (hbm,) * 8,
        scratch_shapes=[
            pltpu.VMEM((4, D, D), F32),
            pltpu.VMEM((2, 1, D, D), F32),
            pltpu.VMEM((8, D), F32),
            pltpu.VMEM((ROWS, D), F32),
            pltpu.VMEM((4, BLK, D), F32),
            pltpu.VMEM((2, HALF, D), F32),
            pltpu.VMEM((2, BLK, D), F32),
            pltpu.VMEM((2, ROWS, D), BF16),
            pltpu.VMEM((2, ROWS, D), BF16),
            pltpu.VMEM((2, ROWS, D), BF16),
            pltpu.VMEM((2, ROWS, 192), BF16),
            pltpu.VMEM((2, ROWS, 192), BF16),
            pltpu.VMEM((2, ROWS, 192), BF16),
            pltpu.VMEM((2, ROWS, 192), BF16),
            pltpu.VMEM((ROWS, D), F32),
            pltpu.VMEM((2, 12, BLK, BLK), F32),
            pltpu.VMEM((2, BLK, D), F32),
            pltpu.VMEM((BLK, D), F32),
            pltpu.VMEM((BLK, D), F32),
            pltpu.VMEM((ROWS, D), BF16),
            pltpu.VMEM((2, ROWS, D), BF16),
            pltpu.VMEM((2, ROWS, D), BF16),
            pltpu.VMEM((2, ROWS, 192), BF16),
            pltpu.VMEM((2, ROWS, 192), BF16),
            pltpu.VMEM((2, ROWS, 192), BF16),
            pltpu.VMEM((3, D, D), BF16),
            pltpu.VMEM((2, D, D), BF16),
            pltpu.VMEM((BLK, D), F32),
            pltpu.VMEM((BLK, D), F32),
            pltpu.VMEM((4, BLK, D), F32),
            pltpu.VMEM((2, BLK, D), F32),
            pltpu.VMEM((3, 1, 48, 384), F32),
            pltpu.VMEM((3, 3, 48, 384), F32),
            pltpu.VMEM((2, 192, 384), F32),
        ] + sum_bufs(2) + sum_bufs(1) + [
            pltpu.VMEM((4, 4, 8, D), F32),
            pltpu.VMEM((4, 4, 2, 8, BLK), F32),
            pltpu.VMEM((4, 4, 2, 8, 256), F32),
        ] + sems(6) + sems(6) + sems(4, 6) + sems(2, 20) + sems(2, 20) + sems(3, 13) + sems(10) + sems(7) + sems(7)
        + [sem((11,)), sem((2,)), sem((2,)), sem((2,)), sem((5,))],
        compiler_params=pltpu.CompilerParams(collective_id=0, has_side_effects=True, vmem_limit_bytes=int(63 * 2 ** 20)),
        name="layers",
    )(tokens, trow, cotangent, ids, wqkv, w_out, w_up, w_down, norm_gain, norm_bias)[:7]
    qkv = att[:, 0, 0:576].reshape(2, 3, 192, D).transpose(0, 3, 1, 2)
    return (lo.astype(BF16), tg, table[:, 0:time_table.shape[0]].T, qkv, att[:, 0, 576:768], mlp[0], mlp[1], gain, bias)


def solution(mesh):
    placed = (
        P("dp", None), P("dp", None), P("dp"), P(), P(None, None, None, "tensor"), P(None, "tensor", None),
        P(None, None, "tensor"), P(None, "tensor", None), P(), P(),
    )
    return jax.shard_map(
        functools.partial(on_device, 4, 4, 4),
        mesh=mesh,
        in_specs=placed,
        out_specs=(
            P("dp", None), P("dp", None), P(None, "tensor"), P(None, None, None, "tensor"), P(None, "tensor", None),
            P(None, None, "tensor"), P(None, "tensor", None), P(), P(),
        ),
        check_vma=False,
    )
```

time: 443 us -> 264 us (0.60)
  blocking collectives: 118 us -> 0 us
  waiting for transfers between devices: 30.1 us -> 0 us
  other arithmetic: 21.6 us -> 4.54 us
  between operations: 14.8 us -> 0.67 us
    psum x1 -> x0, blocking collectives: 79.3 us -> none  [on_device(): vec = lax.psum(vec, ('dp', 'tensor'))]
    psum x1 -> x0, waiting for transfers between devices: 30.1 us -> none  [on_device(): mats = lax.psum(mats, 'dp')]
    all_gather x1 -> x0, blocking collectives: 27.7 us -> none  [on_device(): sums = lax.all_gather(sums, 'dp', axis=0, tiled=True)]
    unnamed x1 -> x0, blocking collectives: 11.1 us -> none
    concatenate x1 -> x0, other arithmetic: 10.5 us -> none  [on_device(): mats = jnp.concatenate([ga0, gm0, ga1, gm1])]
    another operation x3 -> x0, other arithmetic: 8.68 us -> none  [the longest x1 4.34 us: on_device(): up = jnp.stack([mats[1], mats[4]])]
    slice x2 -> x1, local copies, waits for them, and re-layouts: 9.64 us -> 2.03 us  [on_device(): qkv = att[:, 0, 0:576].reshape(2, 3, 192, D).transpose(0, 3, 1, 2)]
    squeeze x0 -> x2, local copies, waits for them, and re-layouts: none -> 6.7 us  [the longest x1 4.34 us: on_device(): mlp[1]]
  transfers between devices with their start and end apart: 1 -> 0, of which waited for: 1 -> 0; matrix products, arithmetic and copies ran while one was open for 1% -> 0% of each run, Pallas kernels for 0% -> 0%
where the time goes in v3:
time: 264 us; the launch traced here: 263 us
  Pallas kernels  239 us (91%)
  local copies, waits for them, and re-layouts  18.8 us (7%)
  other arithmetic  4.54 us (2%)
    pallas_call x1, Pallas kernels, on_device(): pl.pallas_call(functools.partial(body, nz, ny, nx), out_shape=(sd((ROWS,...  239 us

profile of v3, /device:TPU:1, one launch (start us, length us, event | category | flops | bytes accessed | tf_op | source)
XLA Modules:
  0.0 262.9 jit_solution(12058859703413776963)
XLA Ops:
  0.6 0.7 compare_and_fusion
  1.3 0.7 compare_select_fusion
  2.0 1.3 broadcast_in_dim.21.ids_ref
  3.3 2.8 %gather_fusion = bf16[8,768]{1,0:T(8,128)(2,1)S(1)} fusion(bf16[2000,768]{1,0:T(8,128)(2,1)} %param.13, s32[1024]{0:T(1024)S(1)} %pad_clamp_fusion), kind=kCustom, calls=%fused_computation | custom fusion | bytes 24608 | tf_op jit(solution)/shard_map/jit(_take)/gather | solution.py:861
  6.1 0.7 fusion.trow_ref
  6.8 238.8 %layers.1 = (f32[512,768]{1,0:T(8,128)}, f32[512,768]{1,0:T(8,128)}, f32[192,2048]{1,0:T(8,128)}, f32[2,2,768]{2,1,0:T(2,128)}, f32[2,2,768]{2,1,0:T(2,128)}, /*...) custom-call(bf16[512,768]{1,0:T(8,128)(2,1)} %tok_ref.1, ...), custom_call_target="tpu_custom_call" | custom-call | tf_op jit(solution)/shard_map/layers/pallas_call | solution.py:879
  245.7 0.0 copy-start.1
  245.7 2.5 convert_element_type.14
  248.2 2.4 slice_bitcast_fusion.3
  250.6 0.0 copy-done.1
  250.6 0.0 copy-start
  250.6 2.0 slice.16
  252.6 3.4 %slice_bitcast_fusion.2 = f32[2000,192]{0,1:T(8,128)} fusion(f32[192,2048]{1,0:T(8,128)} %get-tuple-element.18), kind=kLoop, calls=%fused_computation.3 | loop fusion | bytes 3072000 | tf_op jit(solution)/shard_map/transpose | solution.py:932
  256.0 0.1 copy-done
  256.2 0.0 copy-start.2
  256.2 4.3 %slice_bitcast_fusion = (f32[2,768,768]{2,1,0:T(8,128)}, f32[2,768,768]{2,1,0:T(8,128)}) fusion(f32[2,2,768,768]{3,2,1,0:T(8,128)S(1)} %copy-done), kind=kLoop, calls=%fused_computation.1 | loop fusion | bytes 18874368 | tf_op jit(solution)/shard_map/squeeze | solution.py:932
  260.5 0.0 copy-start.4
  260.5 0.0 copy-start.3
  260.5 0.0 copy-done.2
  260.5 1.1 copy.26
  261.7 0.0 copy-done.4
  261.7 0.6 copy.27
  262.3 0.0 copy-done.3
  262.3 0.6 copy.28
  (1 shorter events, 0.0 us)
Async XLA Ops:
  245.7 4.9 %copy-start.1 = (f32[2,1,768,768]{3,2,1,0:T(8,128)S(1)}, f32[2,1,768,768]{3,2,1,0:T(8,128)}, u32[]{:S(2)}) copy-start(f32[2,1,768,768]{3,2,1,0:T(8,128)} %get-tuple-element.19) | copy-start | bytes 14155780
  250.6 5.6 %copy-start = (f32[2,2,768,768]{3,2,1,0:T(8,128)S(1)}, f32[2,2,768,768]{3,2,1,0:T(8,128)}, u32[]{:S(2)}) copy-start(f32[2,2,768,768]{3,2,1,0:T(8,128)} %get-tuple-element.20) | copy-start | bytes 28311556
  256.2 4.4 %copy-start.2 = (f32[512,768]{1,0:T(8,128)S(1)}, f32[512,768]{1,0:T(8,128)}, u32[]{:S(2)}) copy-start(f32[512,768]{1,0:T(8,128)} %get-tuple-element.35) | copy-start | bytes 4718596
  260.5 1.2 copy-start.4
  260.5 1.8 copy-start.3
